TPU v7x, 128 devices: a whole 4x4x4 slice. The times are simulated.
128 devices in a mesh: group: 2 (over core), fsdp: 8 (over x, y_hi), tp: 8 (over z, y_lo).
Axes of the slice: x: 4, y: 4 (y_hi: 2, y_lo: 2; y = y_hi * 2 + y_lo), z: 4, core: 2. Of those that a mesh axis runs over, the one named last changes fastest.
Arguments:
- learn_input: bfloat16 [16384, 5120], P(('group', 'fsdp')), may hold values from -8 to 8
- learn_cotangent: bfloat16 [16384, 2, 1024], P(('group', 'fsdp'), None, 'tp'), may hold values from -0.375 to 0.375
- weight: float32 [5120, 2, 1024], P(('group', 'fsdp'), None, 'tp'), may hold values from -0.078125 to 0.078125
- moment: float32 [5120, 2, 1024], P(('group', 'fsdp'), None, 'tp'), may hold values from -6 to 6
- second: float32 [5120, 2, 1024], P(('group', 'fsdp'), None, 'tp'), may hold values from 1 to 10
- table: bfloat16 [77824, 5120], P(('group', 'fsdp'), 'tp'), may hold values from -6 to 6
- gain: bfloat16 [5120], replicated, may hold values from 0.099609375 to 1.8984375
- query_weight: bfloat16 [5120, 8192], P(None, 'tp'), may hold values from -0.078125 to 0.078125
- cache: bfloat16 [2, 32, 8, 4096, 128], P(None, ('group', 'fsdp'), 'tp'), may hold values from -6 to 6
- token_ids: int32 [32, 3], replicated, may hold values from 0 to 77823
- lengths: int32 [32], P(('group', 'fsdp')), may hold values from 1 to 4096
Outputs:
- new_weight: float32 [5120, 2, 1024], P(('group', 'fsdp'), None, 'tp')
- new_moment: float32 [5120, 2, 1024], P(('group', 'fsdp'), None, 'tp')
- new_second: float32 [5120, 2, 1024], P(('group', 'fsdp'), None, 'tp')
- new_kv: bfloat16 [2, 32, 8, 3, 128], P(None, ('group', 'fsdp'), 'tp')
- attended: bfloat16 [32, 3, 8192], P(('group', 'fsdp'), None, 'tp')
All inputs are finite; a program needn't handle non-finite values.
Results may differ from a plain program's by a relative error of at most 0.02.
Values may be sent and summed in bfloat16 or wider, within the bound.
A program may use at most 128 MiB of HBM per device.

v0:
```python
import math

import jax
import jax.numpy as jnp
from jax import lax
from jax.sharding import PartitionSpec as P

QUERY_HEADS = 64
KEY_VALUE_HEADS = 8
HEAD_SIZE = 128
DECODE_STEPS = 3


learn_rate = 0.002
beta_one = 0.9
beta_two = 0.95
bias_one = 1.0 - 0.9**10
bias_two = 1.0 - 0.95**10
adam_eps = 1e-08
weight_decay = 0.1
norm_eps = 1e-06
rope_log = math.log(1000000.0)


def head_norm(values):
    return values * lax.rsqrt(jnp.mean(values * values, axis=-1, keepdims=True) + norm_eps)


def rotate(values, positions):
    half = values.shape[-1] // 2
    freqs = jnp.exp(-rope_log * 2.0 * jnp.arange(half, dtype=jnp.float32) / values.shape[-1])
    angles = positions.astype(jnp.float32)[:, :, None, None] * freqs
    cosine = jnp.cos(angles)
    sine = jnp.sin(angles)
    first = values[..., :half]
    latter = values[..., half:]
    return jnp.concatenate(
        [first * cosine - latter * sine, latter * cosine + first * sine], axis=-1
    )


def shards(
    learn_input,
    learn_cotangent,
    weight,
    moment,
    second,
    table,
    gain,
    query_weight,
    cache,
    token_ids,
    lengths,
):
    tokens, width = learn_input.shape
    rows_own = weight.shape[0]
    kv_cols = weight.shape[2]
    flat_cot = learn_cotangent.reshape(tokens, 2 * kv_cols)
    term = lax.dot_general(
        learn_input, flat_cot, (((0,), (0,)), ((), ())), preferred_element_type=jnp.float32
    )
    grad = lax.psum_scatter(
        term.astype(jnp.bfloat16).astype(jnp.float32).astype(jnp.bfloat16),
        ("group", "fsdp"),
        scatter_dimension=0,
        tiled=True,
    ).astype(jnp.float32)
    grad = grad.reshape(rows_own, 2, kv_cols)
    new_moment = beta_one * moment + (1.0 - beta_one) * grad
    new_second = beta_two * second + (1.0 - beta_two) * grad * grad
    update = new_moment / bias_one / (jnp.sqrt(new_second / bias_two) + adam_eps)
    new_weight = weight - learn_rate * (update + weight_decay * weight)
    fresh_weights = new_weight.astype(jnp.bfloat16)
    vocab_own = table.shape[0]
    owner = lax.axis_index(("group", "fsdp"))
    local_ids = token_ids - owner * vocab_own
    valid = (local_ids >= 0) & (local_ids < vocab_own)
    picked = jnp.take(table, jnp.clip(local_ids, 0, vocab_own - 1), axis=0)
    terms = jnp.where(valid[..., None], picked.astype(jnp.float32), 0.0)
    mine = lax.psum_scatter(
        terms.astype(jnp.bfloat16), ("group", "fsdp"), scatter_dimension=0, tiled=True
    )
    emb = lax.all_gather(mine, "tp", axis=2, tiled=True).astype(jnp.float32)
    rows = emb.shape[0]
    mean_sq = jnp.mean(emb * emb, axis=-1, keepdims=True)
    normed = (emb * gain.astype(jnp.float32) * lax.rsqrt(mean_sq + norm_eps)).astype(jnp.bfloat16)
    flat_layout = normed.reshape(rows * DECODE_STEPS, width)
    heads_kv = kv_cols // HEAD_SIZE
    query_groups = QUERY_HEADS // KEY_VALUE_HEADS
    qraw = jnp.dot(flat_layout, query_weight, preferred_element_type=jnp.float32)
    qraw = qraw.reshape(rows, DECODE_STEPS, heads_kv * query_groups, HEAD_SIZE)
    full = lax.all_gather(fresh_weights, ("group", "fsdp"), axis=0, tiled=True)
    key_value_unshaped = jnp.dot(
        flat_layout, full.reshape(width, 2 * kv_cols), preferred_element_type=jnp.float32
    )
    key_value_unshaped = key_value_unshaped.reshape(rows, DECODE_STEPS, 2, heads_kv, HEAD_SIZE)
    positions = lengths[:, None] + jnp.arange(DECODE_STEPS, dtype=jnp.int32)[None, :]
    query_vectors = rotate(head_norm(qraw), positions).astype(jnp.bfloat16)
    new_keys = rotate(head_norm(key_value_unshaped[:, :, 0]), positions).astype(jnp.bfloat16)
    new_values = key_value_unshaped[:, :, 1].astype(jnp.bfloat16)
    new_kv = jnp.stack([new_keys, new_values]).transpose(0, 1, 3, 2, 4)
    grouped_query = query_vectors.reshape(rows, DECODE_STEPS, heads_kv, query_groups, HEAD_SIZE)
    scale = 1.0 / math.sqrt(HEAD_SIZE)
    old = (
        jnp.einsum("rskgd,rkcd->rskgc", grouped_query, cache[0], preferred_element_type=jnp.float32)
        * scale
    )
    live = jnp.arange(cache.shape[3])[None, :] < lengths[:, None]
    old_w = jnp.where(live[:, None, None, None, :], jnp.exp(old), 0.0)
    recent = (
        jnp.einsum("rskgd,rtkd->rskgt", grouped_query, new_keys, preferred_element_type=jnp.float32)
        * scale
    )
    causal = jnp.arange(DECODE_STEPS)[:, None] >= jnp.arange(DECODE_STEPS)[None, :]
    recent_w = jnp.where(causal[None, :, None, None, :], jnp.exp(recent), 0.0)
    denom = jnp.sum(old_w, axis=-1) + jnp.sum(recent_w, axis=-1)
    numer = jnp.einsum(
        "rskgc,rkcd->rskgd",
        old_w.astype(jnp.bfloat16),
        cache[1],
        preferred_element_type=jnp.float32,
    )
    numer = numer + jnp.einsum(
        "rskgt,rtkd->rskgd",
        recent_w.astype(jnp.bfloat16),
        new_values,
        preferred_element_type=jnp.float32,
    )
    attended = (
        (numer / denom[..., None])
        .astype(jnp.bfloat16)
        .reshape(rows, DECODE_STEPS, heads_kv * query_groups * HEAD_SIZE)
    )
    return (new_weight, new_moment, new_second, new_kv, attended)


def solution(mesh):
    return jax.shard_map(
        shards,
        mesh=mesh,
        in_specs=(
            P(("group", "fsdp"), None),
            P(("group", "fsdp"), None, "tp"),
            P(("group", "fsdp"), None, "tp"),
            P(("group", "fsdp"), None, "tp"),
            P(("group", "fsdp"), None, "tp"),
            P(("group", "fsdp"), "tp"),
            P(),
            P(None, "tp"),
            P(None, ("group", "fsdp"), "tp", None, None),
            P(),
            P(("group", "fsdp")),
        ),
        out_specs=(
            P(("group", "fsdp"), None, "tp"),
            P(("group", "fsdp"), None, "tp"),
            P(("group", "fsdp"), None, "tp"),
            P(None, ("group", "fsdp"), "tp", None, None),
            P(("group", "fsdp"), None, "tp"),
        ),
        check_vma=False,
    )
```

profile of v0, /device:TPU:1, one launch (start us, length us, event | category | flops | bytes accessed | tf_op | source)
XLA Modules:
  0.0 302.7 jit_solution(15786906014753457366)
XLA Ops:
  7.2 8.6 %convolution_convert_fusion = bf16[5120,256]{1,0:T(8,128)(2,1)} fusion(bf16[1024,5120]{1,0:T(8,128)(2,1)} %param.11, bf16[128,8,2,128]{3,2,1,0:T(2,128)(2,1)} %bitcast.128), kind=kOutput, calls=%fused_computation.1 | convolution fusion | flops 2685665280 | bytes 13631488 | tf_op jit(solution)/shard_map/dot_general | solution.py:59
  15.9 0.1 copy.42
  16.0 0.1 reshape.303
  16.1 4.4 %gather_fusion = bf16[96,640]{1,0:T(8,128)(2,1)S(1)} fusion(bf16[4864,640]{1,0:T(8,128)(2,1)} %param.16, s32[1024]{0:T(1024)S(1)} %pad_clamp_fusion), kind=kCustom, calls=%fused_computation | custom fusion | bytes 246144 | tf_op jit(solution)/shard_map/jit(_take)/gather | solution.py:78
  20.6 0.1 copy.40
  20.7 0.1 copy.41
  20.8 0.8 select_convert_fusion
  21.7 69.4 %reduce-scatter.2.cloned.1.call-done = bf16[320,256]{1,0:T(8,128)(2,1)} async-done(((bf16[5120,256]{1,0:T(8,128)(2,1)}), bf16[320,256]{1,0:T(8,128)(2,1)}) %reduce-scatter.2.cloned.1.call-update) | async-done | bytes 163856 | tf_op jit(solution)/shard_map/reduce_scatter | solution.py:62
  91.2 1.1 reshape.300
  92.3 2.1 fusion.48
  94.4 13.7 %copy.58 = bf16[1024,5120]{1,0:T(8,128)(2,1)} copy(bf16[1024,5120]{0,1:T(8,128)(2,1)} %bitcast.121) | data formatting | bytes 20971520 | tf_op jit(solution)/shard_map/dot_general | solution.py:90
  108.2 0.6 dynamic-slice
  109.5 0.1 multiply_cosine_fusion
  109.7 0.1 iota_compare_fusion
  109.8 126.5 %all-reduce.3.cloned.1.call-done = bf16[32,3,640]{2,1,0:T(4,128)(2,1)} async-done(((bf16[32,3,640]{2,1,0:T(4,128)(2,1)}), bf16[32,3,640]{2,1,0:T(4,128)(2,1)}) %all-reduce.3.cloned.1.call-update) | async-done | bytes 122896
  236.2 0.7 constant_dynamic-slice_fusion
  236.9 22.8 %all_gather.6 = bf16[2,3,5120]{2,1,0:T(4,128)(2,1)S(1)} all-gather(bf16[2,3,640]{2,1,0:T(4,128)(2,1)S(1)} %constant_dynamic-slice_fusion), channel_id=1, replica_groups=mesh['group'=2,'fsdp'=8,'tp'=8] {'tp'}, dimensions={2}, use_global_device_ids=true | all-gather | bytes 69120 | tf_op jit(solution)/shard_map/all_gather | solution.py:83
  259.7 0.1 fusion.25
  259.8 5.8 %multiply_reduce_fusion = (f32[2,3,8]{1,2,0:T(8,128)S(1)}, f32[2,3,8,128]{3,1,2,0:T(4,128)S(1)}) fusion(bf16[8,128,5120,1]{2,1,0,3:T(8,128)(2,1)} %bitcast.120, bf16[2,3,5120]{2,1,0:T(4,128)(2,1)S(1)} %all_gather.6, f32[2,3]{1,0:T(2,128)S(1)} %add_rsqrt_fusion.2, f32[5120]{0:T(1024)S(1)} %convert_element_type.82), kind=kOutput, calls=%fused_computation.40 | convolution fusion | flops 63049680 | bytes 10592472 | tf_op jit(solution)/shard_map/dot_general | solution.py:90
  265.8 0.1 subtract_convert_fusion
  265.9 0.1 pad_maximum_fusion
  266.0 0.8 fusion.50
  266.7 0.4 fusion.8
  267.1 20.3 %all-gather.2.cloned.1.call-done = bf16[5120,2,128]{2,1,0:T(2,128)(2,1)} async-done(((bf16[320,2,128]{2,1,0:T(2,128)(2,1)}), bf16[5120,2,128]{2,1,0:T(2,128)(2,1)}) %all-gather.2.cloned.1.call-update) | async-done | bytes 2621456 | tf_op jit(solution)/shard_map/all_gather | solution.py:92
  287.5 5.9 %copy.57 = bf16[5120,2,128]{0,2,1:T(8,128)(2,1)S(1)} copy(bf16[5120,2,128]{2,1,0:T(2,128)(2,1)} %all-gather.2.cloned.1.call-done) | data formatting | bytes 5242880 | tf_op jit(solution)/shard_map/reshape | solution.py:94
  293.3 0.8 fusion.11
  294.1 0.1 multiply_reduce_fusion.1
  294.3 0.1 fusion.36
  294.5 0.2 fusion.51
  294.7 0.2 fusion.17
  294.9 0.6 reshape.298
  295.6 0.6 copy.51
  (38 shorter events, 0.7 us)
Async XLA Ops:
  7.2 84.0 %reduce-scatter.2.cloned.1.call-start = ((), (), s32[]{:S(2)}) async-start(), calls=%async_computation.1 | async-start | bytes 2785280 | tf_op jit(solution)/shard_map/reduce_scatter | solution.py:62
  7.2 8.7 %copy-start.5 = (s32[32,3]{0,1:T(4,128)S(1)}, s32[32,3]{0,1:T(4,128)}, u32[]{:S(2)}) copy-start(s32[32,3]{0,1:T(4,128)} %param.20) | copy-start | bytes 1156
  15.8 76.4 %copy-start.1 = (f32[320,2,128]{2,1,0:T(2,128)S(1)}, f32[320,2,128]{2,1,0:T(2,128)}, u32[]{:S(2)}) copy-start(f32[320,2,128]{2,1,0:T(2,128)} %param.13) | copy-start | bytes 983044
  15.8 76.4 %copy-start.2 = (f32[320,2,128]{2,1,0:T(2,128)S(1)}, f32[320,2,128]{2,1,0:T(2,128)}, u32[]{:S(2)}) copy-start(f32[320,2,128]{2,1,0:T(2,128)} %param.14) | copy-start | bytes 983044
  15.8 76.4 %copy-start.3 = (f32[320,2,128]{2,1,0:T(2,128)S(1)}, f32[320,2,128]{2,1,0:T(2,128)}, u32[]{:S(2)}) copy-start(f32[320,2,128]{2,1,0:T(2,128)} %param.15) | copy-start | bytes 983044
  15.8 78.6 %copy-start.4 = (bf16[5120]{0:T(1024)(128)(2,1)S(1)}, bf16[5120]{0:T(1024)(128)(2,1)}, u32[]{:S(2)}) copy-start(bf16[5120]{0:T(1024)(128)(2,1)} %param.17) | copy-start | bytes 30724
  15.9 220.4 %all-reduce.3.cloned.1.call-start = ((), (), s32[]{:S(2)}) async-start(), calls=%async_computation.3 | async-start | bytes 327680
  21.7 265.8 %all-gather.2.cloned.1.call-start = ((), (), s32[]{:S(2)}) async-start(), calls=%async_computation.2 | async-start | bytes 2785280 | tf_op jit(solution)/shard_map/all_gather | solution.py:92
  94.4 13.8 %copy-start.7 = (u32[128]{0:T(128)S(1)}, u32[128]{0:T(128)}, u32[]{:S(2)}) copy-start(u32[128]{0:T(128)} %constant.78) | copy-start | bytes 1540
  94.4 15.0 %copy-start.6 = (s32[2]{0:T(128)S(1)}, s32[2]{0:T(128)}, u32[]{:S(2)}) copy-start(s32[2]{0:T(128)} %param.21) | copy-start | bytes 28
  259.8 6.1 %copy-start = (bf16[2,2,1,4096,128]{4,3,2,1,0:T(8,128)(2,1)S(1)}, bf16[2,2,1,4096,128]{4,3,2,1,0:T(8,128)(2,1)}, u32[]{:S(2)}) copy-start(bf16[2,2,1,4096,128]{4,3,2,1,0:T(8,128)(2,1)} %param.19) | copy-start | bytes 12582916
Sparse Core Ops, SparseCore 0:
  16.0 75.1 reduce-scatter.1
  93.8 142.3 all-reduce.2
  238.7 48.7 all-gather.1
where the time goes:
time: 303 us
  waiting for transfers between devices  216 us (71%)
  local copies, waits for them, and re-layouts  28.1 us (9%)
  blocking collectives  22.8 us (8%)
  matrix products  16.8 us (6%)
  between operations  14.6 us (5%)
  other arithmetic  4.05 us (1%)
    unnamed x4, waiting for transfers between devices  127 us
    reduce_scatter x1, waiting for transfers between devices, shards(): lax.psum_scatter(term.astype(jnp.bfloat16).astype(jnp.float32).astype(jnp...  69.4 us
    all_gather x1, blocking collectives, shards(): emb = lax.all_gather(mine, 'tp', axis=2, tiled=True).astype(jnp.float32)  22.8 us
    all_gather x1, waiting for transfers between devices, shards(): full = lax.all_gather(fresh_weights, ('group', 'fsdp'), axis=0, tiled=True)  20.3 us
    dot_general x1, local copies, waits for them, and re-layouts, shards(): jnp.dot(flat_layout, query_weight, preferred_element_type=jnp.float32)  13.7 us
    dot_general x1, matrix products, shards(): lax.dot_general(learn_input, flat_cot, (((0,), (0,)), ((), ())), preferre...  8.59 us
  transfers between devices with their start and end apart: 3, of which 3 were waited for; matrix products, arithmetic and copies ran while one was open for 10% of the time, Pallas kernels for 0%

commit v1 on v0

v1 whole, which is shorter than its diff:
```python
import functools
import math

import jax
import jax.numpy as jnp
from jax import lax
from jax.experimental import pallas as pl
from jax.experimental.pallas import tpu as pltpu
from jax.sharding import PartitionSpec as P

MESH = pl.DeviceIdType.MESH
BF16 = jnp.bfloat16
F32 = jnp.float32

WIDTH = 5120
TOK = 1024
HEAD = 128
HEADS = 8
STEPS = 3
VOCAB_OWN = 4864
POSITIONS = 4096
OWN = 320
CHUNK = 640
PAD = 8

learn_rate = 0.002
beta_one = 0.9
beta_two = 0.95
bias_one = 1.0 - 0.9**10
bias_two = 1.0 - 0.95**10
adam_eps = 1e-08
weight_decay = 0.1
norm_eps = 1e-06
rope_log = math.log(1000000.0)


def adam(weight, moment, second, grad):
    new_moment = beta_one * moment + (1.0 - beta_one) * grad
    new_second = beta_two * second + (1.0 - beta_two) * grad * grad
    update = new_moment / bias_one / (jnp.sqrt(new_second / bias_two) + adam_eps)
    new_weight = weight - learn_rate * (update + weight_decay * weight)
    return new_weight, new_moment, new_second


def head_norm(values):
    return values * lax.rsqrt(jnp.mean(values * values, axis=-1, keepdims=True) + norm_eps)


def kernel(
    li_hbm,
    cot_hbm,
    w_hbm,
    m_hbm,
    v_hbm,
    table_hbm,
    gain_ref,
    qw_hbm,
    cache_hbm,
    ids_ref,
    cos_ref,
    sin_ref,
    len_ref,
    grad_ref,
    kv_ref,
    att_ref,
    li,
    cot,
    cotf,
    cot_t,
    wm,
    table,
    qw,
    cache,
    core_send,
    core_recv,
    own,
    part,
    recv1,
    send2,
    recv2,
    send3,
    recv3,
    e1_pick,
    e1a_recv,
    e1_sum,
    e1b_recv,
    e2,
    tiles,
    normed,
    qraw,
    e3_send,
    e3_recv,
    fresh,
    kv_send,
    kv_recv,
    load_sem,
    core_sem,
    s1_sem,
    s2_sem,
    s3_sem,
    e1a_sem,
    e1b_sem,
    e2_sem,
    e3_sem,
    kv_sem,
):
    c, f, t = lax.axis_index("group"), lax.axis_index("fsdp"), lax.axis_index("tp")
    x, h = f // 2, f % 2
    gf = c * 8 + f
    other_c = 1 - c
    near_a = x + 1 - 2 * (x % 2)
    near_b = 3 - x
    far = (x + 2) % 4
    order = (far, near_a, near_b, x)

    core_peer = (other_c, f, t)
    a_peer = (c, near_a * 2 + h, t)
    b_peer = (c, near_b * 2 + h, t)
    h_peer = (c, x * 2 + 1 - h, t)

    def gf_peer(d):
        there = (gf + d) % 16
        return (there // 8, there % 8, t)

    def f_peer(d):
        return (c, (f + d) % 8, t)

    def tp_peer(d):
        return (c, f, (t + d) % 8)

    def remote(src, dst, sems, index, peer):
        return pltpu.make_async_remote_copy(
            src_ref=src,
            dst_ref=dst,
            send_sem=sems.at[(0,) + index],
            recv_sem=sems.at[(1,) + index],
            device_id=peer,
            device_id_type=MESH,
        )

    def load(src, dst, n):
        return pltpu.make_async_copy(src, dst, load_sem.at[n])

    def li_load(j):
        core = other_c if j % 2 == 0 else c
        column = pl.multiple_of(core * 2560 + order[j // 2] * CHUNK, 128)
        return load(li_hbm.at[:, pl.ds(column, CHUNK)], li.at[j], j)

    cot_load = load(cot_hbm, cot, 8)
    table_load = load(table_hbm, table, 9)
    w_loads = [load(ref, wm.at[n], 10 + n) for n, ref in enumerate((w_hbm, m_hbm, v_hbm))]
    qw_load = load(qw_hbm, qw, 13)
    cache_load = load(cache_hbm, cache, 14)

    cot_load.start()
    li_load(0).start()
    li_load(1).start()
    table_load.start()
    for j in range(2, 8):
        li_load(j).start()

    barrier = pltpu.get_barrier_semaphore()
    for d in range(1, 16):
        pl.semaphore_signal(barrier, inc=1, device_id=gf_peer(d), device_id_type=MESH)
    for d in range(1, 8):
        pl.semaphore_signal(barrier, inc=1, device_id=tp_peer(d), device_id_type=MESH)

    cot_load.wait()
    cotf[...] = cot[...].astype(F32)
    for n in range(2):
        cot_t[pl.ds(n * HEAD, HEAD), :] = cotf[pl.ds(n, TOK, 2), :].T.astype(BF16)

    def term(j):
        li_load(j).wait()
        return jnp.dot(cot_t[...], li[j], preferred_element_type=F32).T

    def core_copy(i):
        return remote(core_send.at[i], core_recv.at[i], core_sem, (i,), core_peer)

    def terms(i):
        core_send[i] = term(2 * i).astype(BF16)
        if i == 0:
            pl.semaphore_wait(barrier, 22)
        core_copy(i).start()
        own[i] = term(2 * i + 1)

    def add_cores(i):
        core_copy(i).wait_recv()
        for ab in range(2):
            lanes = pl.ds(ab * HEAD, HEAD)
            part[i, ab] = (own[i, :, lanes] + core_recv[i, :, lanes].astype(F32)).astype(BF16)

    def half(way):
        return pl.ds(pl.multiple_of((1 - h if way == 0 else h) * OWN, 64), OWN)

    peers = (a_peer, b_peer)

    def step1(i, ab, slot, way):
        return remote(
            part.at[i, ab, half(way)], recv1.at[ab, slot, way], s1_sem, (ab, slot, way), peers[ab]
        )

    def step2(ab, way):
        return remote(
            send2.at[ab, way], recv2.at[ab, way], s2_sem, (ab, way), peers[1 - ab]
        )

    def step2_go(way):
        for ab, i in ((0, 2), (1, 1)):
            step1(i, ab, 0, way).wait_recv()
            send2[ab, way] = (
                part[i, ab, half(way)].astype(F32) + recv1[ab, 0, way].astype(F32)
            ).astype(BF16)
            step2(ab, way).start()

    def step3(ab):
        return remote(send3.at[ab], recv3.at[ab], s3_sem, (ab,), h_peer)

    def x_sum(ab, way):
        step1(3, ab, 1, way).wait_recv()
        step2(ab, way).wait_recv()
        return (
            part[3, ab, half(way)].astype(F32)
            + recv1[ab, 1, way].astype(F32)
            + recv2[ab, way].astype(F32)
        )

    terms(0)

    table_load.wait()
    local = ids_ref[...] - gf * VOCAB_OWN
    hot = jnp.where(
        lax.broadcasted_iota(jnp.int32, (16 * PAD, VOCAB_OWN), 1) == local, 1.0, 0.0
    ).astype(BF16)
    picked = jnp.dot(hot, table[...], preferred_element_type=F32)
    blank = jnp.zeros((PAD, HEAD), F32)
    for device in range(16):
        rows = picked[device * PAD : (device + 1) * PAD]
        e1_pick[device // 8, device % 8] = jnp.concatenate(
            [rows[:, b * HEAD : (b + 1) * HEAD] for b in range(5)] + [blank], axis=0
        ).astype(BF16)
    e1a = remote(e1_pick.at[other_c], e1a_recv, e1a_sem, (), core_peer)
    e1a.start()

    terms(1)
    add_cores(0)
    for way in range(2):
        step1(0, 0, 0, way).start()
        step1(0, 1, 0, way).start()

    e1a.wait_recv()
    e1_sum[...] = (e1_pick[c].astype(F32) + e1a_recv[...].astype(F32)).astype(BF16)

    def e1b(d):
        return remote(e1_sum.at[(f + d) % 8], e1b_recv.at[d], e1b_sem, (d,), f_peer(d))

    for d in range(1, 8):
        e1b(d).start()

    qw_load.start()
    terms(2)
    add_cores(1)
    for way in range(2):
        step1(1, 0, 1, way).start()
    cache_load.start()
    terms(3)
    add_cores(2)
    for way in range(2):
        step1(2, 1, 1, way).start()
    for one in w_loads:
        one.start()

    mine = e1_sum[f].astype(F32)
    for d in range(1, 8):
        e1b(d).wait_recv()
        mine = mine + e1b_recv[d].astype(F32)
    e2[t] = mine.astype(BF16)

    def e2_copy(d):
        return remote(e2.at[t], e2.at[t], e2_sem, (d,), tp_peer(d))

    def e2_arrival(d):
        there = (t + 8 - d) % 8
        return remote(e2.at[there], e2.at[there], e2_sem, (d,), tp_peer(d))

    for d in range(1, 8):
        e2_copy(d).start()

    add_cores(3)
    step2_go(0)

    for d in range(1, 8):
        e2_arrival(d).wait_recv()
    square = jnp.zeros((PAD, HEAD), F32)
    for n in range(8):
        emb = e2[n].astype(F32)
        for b in range(5):
            one = emb[b * PAD : (b + 1) * PAD]
            square = square + one * one
    mean = jnp.sum(square, axis=-1, keepdims=True) * (1.0 / WIDTH)
    factor = lax.rsqrt(mean + norm_eps)
    for n in range(8):
        emb = e2[n].astype(F32)
        for b in range(5):
            k = n * 5 + b
            one = emb[b * PAD : (b + 1) * PAD] * gain_ref[:, pl.ds(k * HEAD, HEAD)] * factor
            one = one.astype(BF16).astype(F32)
            tiles[pl.ds(k * PAD, PAD), :] = one
            normed[:, pl.ds(k * HEAD, HEAD)] = one
    tiles[pl.ds(40 * PAD, 2 * PAD), :] = jnp.zeros((2 * PAD, HEAD), F32)

    def e3_block(device):
        first = (device // 2) * 5 + 2 * (device % 2)
        return tiles[pl.ds(pl.multiple_of(first * PAD, PAD), 4 * PAD), :].astype(BF16)

    def e3(d):
        return remote(e3_send.at[d], e3_recv.at[d], e3_sem, (d,), gf_peer(d))

    for d in range(1, 16):
        e3_send[d] = e3_block((gf + d) % 16)
        e3(d).start()
    e3_recv[0] = e3_block(gf)

    step2_go(1)

    qw_load.wait()
    normed16 = normed[...].astype(BF16)

    @pl.loop(0, 4)
    def _(n):
        columns = pl.ds(pl.multiple_of(n * 256, 256), 256)
        qraw[:, columns] = jnp.dot(normed16, qw[:, columns], preferred_element_type=F32)

    cosine, sine = cos_ref[...], sin_ref[...]

    def rotate(values):
        return values * cosine + pltpu.roll(values, HEAD // 2, 1) * sine

    query = jnp.concatenate(
        [rotate(head_norm(qraw[:, g * HEAD : (g + 1) * HEAD])) for g in range(HEADS)], axis=0
    ).astype(BF16)

    for ab in range(2):
        send3[ab] = x_sum(ab, 0).astype(BF16)
        step3(ab).start()

    scale = 1.0 / math.sqrt(HEAD)
    cache_load.wait()
    block = 1024
    sums = []
    for r in range(2):
        length = len_ref[r]

        def attend(n, carry, r=r, length=length):
            denom, numer = carry
            where = pl.ds(pl.multiple_of(n * block, block), block)
            scores = lax.dot_general(
                query, cache[0, r, where, :], (((1,), (1,)), ((), ())), preferred_element_type=F32
            )
            position = lax.broadcasted_iota(jnp.int32, scores.shape, 1) + n * block
            weights = jnp.where(position < length, jnp.exp(scores * scale), 0.0)
            denom = denom + jnp.sum(weights, axis=-1, keepdims=True)
            numer = numer + jnp.dot(
                weights.astype(BF16), cache[1, r, where, :], preferred_element_type=F32
            )
            return denom, numer

        rows = HEADS * PAD
        sums.append(
            lax.fori_loop(
                0,
                POSITIONS // block,
                attend,
                (jnp.zeros((rows, 1), F32), jnp.zeros((rows, HEAD), F32)),
            )
        )
    token = lax.broadcasted_iota(jnp.int32, (HEADS * PAD, 1), 0) % PAD
    first_row = token < STEPS
    denom = jnp.where(first_row, sums[0][0], sums[1][0])
    numer = jnp.where(first_row, sums[0][1], sums[1][1])

    for d in range(1, 16):
        e3(d).wait_recv()
    arrived = [e3_recv[d].astype(F32) for d in range(16)]
    features = jnp.concatenate(
        [
            jnp.concatenate([one[b * PAD : (b + 1) * PAD] for one in arrived], axis=0)
            for b in range(3)
        ],
        axis=1,
    ).astype(BF16)

    fresh[...] = jnp.zeros_like(fresh)
    for one in w_loads:
        one.wait()
    for ab in range(2):
        total = x_sum(ab, 1)
        step3(ab).wait_recv()
        total = total + recv3[ab].astype(F32)
        every = pl.ds(ab, OWN, 2)
        grad_ref[every, :] = total
        new_weight, _, _ = adam(wm[0, every, :], wm[1, every, :], wm[2, every, :], total)
        fresh[pl.ds(pl.multiple_of(h * 64, 64), OWN), pl.ds(ab * HEAD, HEAD)] = new_weight.astype(
            BF16
        )
    partial = jnp.dot(features, fresh[...], preferred_element_type=F32)

    def kv(d):
        return remote(kv_send.at[d], kv_recv.at[d], kv_sem, (d,), gf_peer(16 - d))

    for d in range(1, 16):
        rows = partial[d * PAD : (d + 1) * PAD]
        kv_send[d] = jnp.concatenate([rows[:, :HEAD], rows[:, HEAD:]], axis=0).astype(BF16)
        kv(d).start()
    total = jnp.concatenate([partial[:PAD, :HEAD], partial[:PAD, HEAD:]], axis=0)
    for d in range(1, 16):
        kv(d).wait_recv()
        total = total + kv_recv[d].astype(F32)
    new_key = rotate(head_norm(total[:PAD])).astype(BF16).astype(F32)
    new_value = total[PAD:].astype(BF16).astype(F32)
    kv_ref[0] = new_key
    kv_ref[1] = new_value

    query32 = query.astype(F32)
    for j in range(2 * STEPS):
        score = jnp.sum(query32 * new_key[j : j + 1], axis=-1, keepdims=True) * scale
        seen = (token // STEPS == j // STEPS) & (token >= j)
        weight = jnp.where(seen, jnp.exp(score), 0.0)
        denom = denom + weight
        numer = numer + weight.astype(BF16).astype(F32) * new_value[j : j + 1]
    attended = numer / denom
    for g in range(HEADS):
        att_ref[:, pl.ds(g * HEAD, HEAD)] = attended[g * PAD : (g + 1) * PAD]

    for i in range(4):
        core_copy(i).wait_send()
    for way in range(2):
        for ab in range(2):
            step1(0, ab, 0, way).wait_send()
            step1(1 + ab, ab, 1, way).wait_send()
            step2(ab, way).wait_send()
    for ab in range(2):
        step3(ab).wait_send()
    e1a.wait_send()
    for d in range(1, 8):
        e1b(d).wait_send()
        e2_copy(d).wait_send()
    for d in range(1, 16):
        e3(d).wait_send()
        kv(d).wait_send()


def shards(
    learn_input,
    learn_cotangent,
    weight,
    moment,
    second,
    table,
    gain,
    query_weight,
    cache,
    token_ids,
    lengths,
):
    rows = lengths.shape[0]
    tokens = rows * STEPS

    ids = jnp.pad(token_ids.reshape(16, tokens), ((0, 0), (0, PAD - tokens)), constant_values=-1)
    ids = ids.reshape(16 * PAD, 1)
    positions = (lengths[:, None] + jnp.arange(STEPS, dtype=jnp.int32)[None, :]).reshape(tokens, 1)
    half = HEAD // 2
    freqs = jnp.exp(-rope_log * 2.0 * jnp.arange(half, dtype=F32) / HEAD)
    angles = positions.astype(F32) * freqs
    angles = jnp.pad(angles, ((0, PAD - tokens), (0, 0)))
    cosine, sine = jnp.cos(angles), jnp.sin(angles)
    cosine = jnp.concatenate([cosine, cosine], axis=1)
    sine = jnp.concatenate([-sine, sine], axis=1)

    anywhere = pl.BlockSpec(memory_space=pl.ANY)
    vmem = pl.BlockSpec(memory_space=pltpu.VMEM)
    smem = pl.BlockSpec(memory_space=pltpu.SMEM)
    dma = pltpu.SemaphoreType.DMA
    grad, kv, att = pl.pallas_call(
        kernel,
        out_shape=(
            jax.ShapeDtypeStruct((2 * OWN, HEAD), F32),
            jax.ShapeDtypeStruct((2, PAD, HEAD), F32),
            jax.ShapeDtypeStruct((PAD, HEADS * HEAD), F32),
        ),
        in_specs=[anywhere] * 6 + [vmem] + [anywhere] * 2 + [vmem] * 3 + [smem],
        out_specs=(vmem, vmem, vmem),
        scratch_shapes=[
            pltpu.VMEM((8, TOK, CHUNK), BF16),
            pltpu.VMEM((2 * TOK, HEAD), BF16),
            pltpu.VMEM((2 * TOK, HEAD), F32),
            pltpu.VMEM((2 * HEAD, TOK), BF16),
            pltpu.VMEM((3, 2 * OWN, HEAD), F32),
            pltpu.VMEM((VOCAB_OWN, CHUNK), BF16),
            pltpu.VMEM((WIDTH, HEADS * HEAD), BF16),
            pltpu.VMEM((2, 2, POSITIONS, HEAD), BF16),
            pltpu.VMEM((4, CHUNK, 2 * HEAD), BF16),
            pltpu.VMEM((4, CHUNK, 2 * HEAD), BF16),
            pltpu.VMEM((4, CHUNK, 2 * HEAD), F32),
            pltpu.VMEM((4, 2, CHUNK, HEAD), BF16),
            pltpu.VMEM((2, 2, 2, OWN, HEAD), BF16),
            pltpu.VMEM((2, 2, OWN, HEAD), BF16),
            pltpu.VMEM((2, 2, OWN, HEAD), BF16),
            pltpu.VMEM((2, OWN, HEAD), BF16),
            pltpu.VMEM((2, OWN, HEAD), BF16),
            pltpu.VMEM((2, 8, 6 * PAD, HEAD), BF16),
            pltpu.VMEM((8, 6 * PAD, HEAD), BF16),
            pltpu.VMEM((8, 6 * PAD, HEAD), BF16),
            pltpu.VMEM((8, 6 * PAD, HEAD), BF16),
            pltpu.VMEM((8, 6 * PAD, HEAD), BF16),
            pltpu.VMEM((42 * PAD, HEAD), F32),
            pltpu.VMEM((PAD, WIDTH), F32),
            pltpu.VMEM((PAD, HEADS * HEAD), F32),
            pltpu.VMEM((16, 4 * PAD, HEAD), BF16),
            pltpu.VMEM((16, 4 * PAD, HEAD), BF16),
            pltpu.VMEM((3 * HEAD, 2 * HEAD), BF16),
            pltpu.VMEM((16, 2 * PAD, HEAD), BF16),
            pltpu.VMEM((16, 2 * PAD, HEAD), BF16),
            dma((15,)),
            dma((2, 4)),
            dma((2, 2, 2, 2)),
            dma((2, 2, 2)),
            dma((2, 2)),
            dma((2,)),
            dma((2, 8)),
            dma((2, 8)),
            dma((2, 16)),
            dma((2, 16)),
        ],
        compiler_params=pltpu.CompilerParams(
            collective_id=0, has_side_effects=True, vmem_limit_bytes=60 * 1024 * 1024
        ),
        name="step",
    )(
        learn_input,
        learn_cotangent.reshape(2 * TOK, HEAD),
        weight.reshape(2 * OWN, HEAD),
        moment.reshape(2 * OWN, HEAD),
        second.reshape(2 * OWN, HEAD),
        table,
        gain.astype(F32).reshape(1, WIDTH),
        query_weight,
        cache.reshape(2, rows, POSITIONS, HEAD),
        ids,
        cosine,
        sine,
        lengths,
    )
    new_weight, new_moment, new_second = adam(
        weight, moment, second, grad.reshape(OWN, 2, HEAD)
    )
    new_kv = kv[:, :tokens].reshape(2, rows, 1, STEPS, HEAD).astype(BF16)
    attended = att[:tokens].reshape(rows, STEPS, HEADS * HEAD).astype(BF16)
    return new_weight, new_moment, new_second, new_kv, attended


def solution(mesh):
    return jax.shard_map(
        shards,
        mesh=mesh,
        in_specs=(
            P(("group", "fsdp"), None),
            P(("group", "fsdp"), None, "tp"),
            P(("group", "fsdp"), None, "tp"),
            P(("group", "fsdp"), None, "tp"),
            P(("group", "fsdp"), None, "tp"),
            P(("group", "fsdp"), "tp"),
            P(),
            P(None, "tp"),
            P(None, ("group", "fsdp"), "tp", None, None),
            P(),
            P(("group", "fsdp")),
        ),
        out_specs=(
            P(("group", "fsdp"), None, "tp"),
            P(("group", "fsdp"), None, "tp"),
            P(("group", "fsdp"), None, "tp"),
            P(None, ("group", "fsdp"), "tp", None, None),
            P(("group", "fsdp"), None, "tp"),
        ),
        check_vma=False,
    )
```

time: 303 us -> 51.5 us (0.17)
  waiting for transfers between devices: 216 us -> 0 us
  Pallas kernels: 0 us -> 40.4 us
  local copies, waits for them, and re-layouts: 28.1 us -> 4.33 us
  blocking collectives: 22.8 us -> 0 us
  matrix products: 16.8 us -> 0 us
  between operations: 14.6 us -> 0.65 us
    unnamed x4 -> x0, waiting for transfers between devices: 127 us -> none
    reduce_scatter x1 -> x0, waiting for transfers between devices: 69.4 us -> none  [shards(): lax.psum_scatter(term.astype(jnp.bfloat16).astype(jnp.float32).astype(jnp...]
    pallas_call x0 -> x1, Pallas kernels: none -> 40.4 us  [shards(): pl.pallas_call(kernel, out_shape=(jax.ShapeDtypeStruct((2 * OWN, HEAD), F...]
    all_gather x1 -> x0, blocking collectives: 22.8 us -> none  [shards(): emb = lax.all_gather(mine, 'tp', axis=2, tiled=True).astype(jnp.float32)]
    all_gather x1 -> x0, waiting for transfers between devices: 20.3 us -> none  [shards(): full = lax.all_gather(fresh_weights, ('group', 'fsdp'), axis=0, tiled=True)]
    dot_general x7 -> x0, matrix products: 16.8 us -> none  [the longest x1 8.59 us: shards(): lax.dot_general(learn_input, flat_cot, (((0,), (0,)), ((), ())), preferre...]
    dot_general x1 -> x0, local copies, waits for them, and re-layouts: 13.7 us -> none  [shards(): jnp.dot(flat_layout, query_weight, preferred_element_type=jnp.float32)]
    reshape x3 -> x2, local copies, waits for them, and re-layouts: 7.55 us -> 0.78 us  [the longest x1 0.71 us: shards(): ids = ids.reshape(16 * PAD, 1)]
  transfers between devices with their start and end apart: 3 -> 0, of which waited for: 3 -> 0; matrix products, arithmetic and copies ran while one was open for 10% -> 0% of each run, Pallas kernels for 0% -> 0%
where the time goes in v1:
time: 51.5 us; the launch traced here: 51.2 us
  Pallas kernels  40.4 us (78%)
  other arithmetic  5.82 us (11%)
  local copies, waits for them, and re-layouts  4.33 us (8%)
  between operations  0.65 us (1%)
    pallas_call x1, Pallas kernels, shards(): pl.pallas_call(kernel, out_shape=(jax.ShapeDtypeStruct((2 * OWN, HEAD), F...  40.4 us
    sub x1, other arithmetic, adam(): new_weight = weight - learn_rate * (update + weight_decay * weight)  2.97 us
    unnamed x9, local copies, waits for them, and re-layouts  1.97 us
    reshape x1, other arithmetic, shards(): gain.astype(F32).reshape(1, WIDTH)  1.31 us

profile of v1, /device:TPU:1, one launch (start us, length us, event | category | flops | bytes accessed | tf_op | source)
XLA Modules:
  0.0 51.2 jit_solution(16875396306454896950)
XLA Ops:
  0.6 0.7 %add_convert_fusion = f32[2,3]{1,0:T(2,128)S(1)} fusion(s32[2]{0:T(128)} %len_ref.1), kind=kLoop, calls=%fused_computation.11 | loop fusion | flops 12 | bytes 32 | tf_op jit(solution)/shard_map/convert_element_type | solution.py:474
  1.4 0.1 convert_element_type.31
  1.5 0.1 broadcast_multiply_fusion
  1.6 0.7 %pad_maximum_fusion = (f32[8,128]{1,0:T(8,128)}, f32[8,128]{1,0:T(8,128)}) fusion(f32[8,64]{1,0:T(8,128)S(1)} %get-tuple-element.26, f32[8,64]{1,0:T(8,128)S(1)} %get-tuple-element.25, f32[8,64]{1,0:T(8,128)S(1)} %get-tuple-element.24), kind=kLoop, calls=%fused_computation.6 | loop fusion | flops 2048 | bytes 14336 | tf_op jit(solution)/shard_map/concatenate | solution.py:477
  2.3 0.8 %copy.20 = s32[32,3]{1,0:T(8,128)S(1)} copy(s32[32,3]{0,1:T(4,128)} %param.20) | data formatting | bytes 768 | tf_op args[9]
  3.0 0.1 reshape.85
  3.1 1.3 %reshape.88 = f32[5120]{0:T(1024)} convert(bf16[5120]{0:T(1024)(128)(2,1)} %param.17) | non-fusion elementwise | flops 5120 | bytes 30720 | tf_op jit(solution)/shard_map/reshape | solution.py:546
  4.4 0.7 %reshape.90.ids_ref = s32[128,1]{1,0:T(8,128)} reshape(s32[16,8]{1,0:T(8,128)S(1)} %pad.8) | data formatting | bytes 1024 | tf_op jit(solution)/shard_map/reshape | solution.py:470
  5.1 0.0 copy-start
  5.1 0.0 copy-start.1
  5.1 0.0 copy-start.2
  5.1 40.4 %step.1 = (f32[640,128]{1,0:T(8,128)}, f32[2,8,128]{2,1,0:T(8,128)}, f32[8,1024]{1,0:T(8,128)}) custom-call(bf16[1024,5120]{1,0:T(8,128)(2,1)} %li_hbm.1, bf16[2048,128]{1,0:T(8,128)(2,1)} %bitcast.12, f32[640,128]{1,0:T(8,128)} %bitcast.9, f32[640,128]{1,0:T(8,128)} %bitcast.10, f32[640,128]{1,0:T(8,128)} %bitcast.11, bf16[4864,640]{1,0:T(8,128)(2,1)} %table_hbm.1, ...), custom_call_target="tpu_custom_call" | custom-call | tf_op jit(solution)/shard_map/step/pallas_call | solution.py:484
  45.5 0.7 %slice.15 = bf16[2,6,128]{2,1,0:T(8,128)(2,1)S(1)} slice(f32[2,8,128]{2,1,0:T(8,128)} %get-tuple-element.9), slice={[0:2], [0:6], [0:128]} | slice | bytes 6144 | tf_op jit(solution)/shard_map/slice | solution.py:557
  46.2 0.6 %copy.23 = bf16[2,2,1,3,128]{4,1,3,2,0:T(2,128)(2,1)} copy(bf16[2,2,1,3,128]{4,0,3,1,2:T(2,128)(2,1)S(1)} %bitcast.15) | data formatting | bytes 6144
  46.8 0.8 %slice.14 = bf16[6,1024]{1,0:T(8,128)(2,1)S(1)} slice(f32[8,1024]{1,0:T(8,128)} %get-tuple-element.10), slice={[0:6], [0:1024]} | slice | bytes 24576 | tf_op jit(solution)/shard_map/slice | solution.py:558
  47.6 0.6 %copy.24 = bf16[2,3,1024]{2,0,1:T(2,128)(2,1)} copy(bf16[2,3,1024]{2,1,0:T(4,128)(2,1)S(1)} %convert_element_type.33) | data formatting | bytes 24576
  48.2 0.0 copy-done
  48.2 0.0 copy-done.1
  48.2 0.0 copy-done.2
  48.2 3.0 %multiply_subtract_fusion = (f32[320,2,128]{2,1,0:T(2,128)}, f32[320,2,128]{2,1,0:T(2,128)}, f32[320,2,128]{2,1,0:T(2,128)}) fusion(f32[320,2,128]{2,1,0:T(2,128)S(1)} %copy-done, f32[320,2,128]{2,1,0:T(2,128)} %bitcast.13, f32[320,2,128]{2,1,0:T(2,128)S(1)} %copy-done.1, f32[320,2,128]{2,1,0:T(2,128)S(1)} %copy-done.2), kind=kLoop, calls=%fused_computation.2 | loop fusion | flops 1228800 | bytes 2293760 | tf_op jit(solution)/shard_map/sub | solution.py:41
  (5 shorter events, 0.1 us)
Async XLA Ops:
  5.1 43.1 %copy-start = (f32[320,2,128]{2,1,0:T(2,128)S(1)}, f32[320,2,128]{2,1,0:T(2,128)}, u32[]{:S(2)}) copy-start(f32[320,2,128]{2,1,0:T(2,128)} %param.13) | copy-start | bytes 983044
  5.1 43.1 %copy-start.1 = (f32[320,2,128]{2,1,0:T(2,128)S(1)}, f32[320,2,128]{2,1,0:T(2,128)}, u32[]{:S(2)}) copy-start(f32[320,2,128]{2,1,0:T(2,128)} %param.14) | copy-start | bytes 983044
  5.1 43.1 %copy-start.2 = (f32[320,2,128]{2,1,0:T(2,128)S(1)}, f32[320,2,128]{2,1,0:T(2,128)}, u32[]{:S(2)}) copy-start(f32[320,2,128]{2,1,0:T(2,128)} %param.15) | copy-start | bytes 983044

commit v2 on v1

--- a/solution.py
+++ b/solution.py
@@ -53,14 +53,12 @@
     m_hbm,
     v_hbm,
     table_hbm,
-    gain_ref,
+    gain_hbm,
     qw_hbm,
     cache_hbm,
-    ids_ref,
-    cos_ref,
-    sin_ref,
-    len_ref,
-    grad_ref,
+    ids_hbm,
+    len_hbm,
+    grad_hbm,
     kv_ref,
     att_ref,
     li,
@@ -80,26 +78,26 @@
     recv2,
     send3,
     recv3,
-    e1_pick,
-    e1a_recv,
-    e1_sum,
-    e1b_recv,
+    e1_send,
+    e1_recv,
     e2,
-    tiles,
-    normed,
+    scaled,
     qraw,
-    e3_send,
     e3_recv,
     fresh,
     kv_send,
     kv_recv,
+    gain,
+    gain32,
+    ids,
+    len_ref,
+    grad,
     load_sem,
     core_sem,
     s1_sem,
     s2_sem,
     s3_sem,
-    e1a_sem,
-    e1b_sem,
+    e1_sem,
     e2_sem,
     e3_sem,
     kv_sem,
@@ -122,9 +120,6 @@
         there = (gf + d) % 16
         return (there // 8, there % 8, t)
 
-    def f_peer(d):
-        return (c, (f + d) % 8, t)
-
     def tp_peer(d):
         return (c, f, (t + d) % 8)
 
@@ -152,11 +147,13 @@
     qw_load = load(qw_hbm, qw, 13)
     cache_load = load(cache_hbm, cache, 14)
 
+    small_loads = [load(ids_hbm, ids, 15), load(len_hbm, len_ref, 16), load(gain_hbm, gain, 17)]
+
     cot_load.start()
-    li_load(0).start()
-    li_load(1).start()
+    for one in small_loads:
+        one.start()
     table_load.start()
-    for j in range(2, 8):
+    for j in range(8):
         li_load(j).start()
 
     barrier = pltpu.get_barrier_semaphore()
@@ -182,6 +179,9 @@
         if i == 0:
             pl.semaphore_wait(barrier, 22)
         core_copy(i).start()
+        if i == 0:
+            for d in range(1, 16):
+                e1(d).start()
         own[i] = term(2 * i + 1)
 
     def add_cores(i):
@@ -225,56 +225,97 @@
             + recv2[ab, way].astype(F32)
         )
 
-    terms(0)
-
+    for one in small_loads:
+        one.wait()
+    slot = lax.broadcasted_iota(jnp.int32, (16 * PAD, 32), 0)
+    row = lax.broadcasted_iota(jnp.int32, (16 * PAD, 32), 1)
+    place = slot % PAD
+    mine = row == 2 * (slot // PAD) + place % 2
+    wanted = jnp.zeros((16 * PAD, 32), F32)
+    for step in range(STEPS):
+        here = mine & (place // 2 == step)
+        wanted = wanted + jnp.where(here, ids[step : step + 1, :].astype(F32), 0.0)
+    wanted = jnp.sum(wanted, axis=-1, keepdims=True).astype(jnp.int32)
+    wanted = jnp.where(place[:, :1] < 2 * STEPS, wanted, -1)
+    hot = jnp.where(
+        lax.broadcasted_iota(jnp.int32, (16 * PAD, VOCAB_OWN), 1) == wanted - gf * VOCAB_OWN, 1.0, 0.0
+    ).astype(BF16)
     table_load.wait()
-    local = ids_ref[...] - gf * VOCAB_OWN
-    hot = jnp.where(
-        lax.broadcasted_iota(jnp.int32, (16 * PAD, VOCAB_OWN), 1) == local, 1.0, 0.0
-    ).astype(BF16)
     picked = jnp.dot(hot, table[...], preferred_element_type=F32)
     blank = jnp.zeros((PAD, HEAD), F32)
     for device in range(16):
         rows = picked[device * PAD : (device + 1) * PAD]
-        e1_pick[device // 8, device % 8] = jnp.concatenate(
+        e1_send[device] = jnp.concatenate(
             [rows[:, b * HEAD : (b + 1) * HEAD] for b in range(5)] + [blank], axis=0
         ).astype(BF16)
-    e1a = remote(e1_pick.at[other_c], e1a_recv, e1a_sem, (), core_peer)
-    e1a.start()
-
+
+    def e1(d):
+        return remote(e1_send.at[(gf + d) % 16], e1_recv.at[d], e1_sem, (d,), gf_peer(d))
+
+    terms(0)
+    qw_load.start()
     terms(1)
     add_cores(0)
-    for way in range(2):
-        step1(0, 0, 0, way).start()
-        step1(0, 1, 0, way).start()
-
-    e1a.wait_recv()
-    e1_sum[...] = (e1_pick[c].astype(F32) + e1a_recv[...].astype(F32)).astype(BF16)
-
-    def e1b(d):
-        return remote(e1_sum.at[(f + d) % 8], e1b_recv.at[d], e1b_sem, (d,), f_peer(d))
-
-    for d in range(1, 8):
-        e1b(d).start()
-
-    qw_load.start()
+    step1(0, 0, 0, 0).start()
+    step1(0, 1, 0, 0).start()
+    cache_load.start()
+    for one in w_loads:
+        one.start()
     terms(2)
     add_cores(1)
-    for way in range(2):
-        step1(1, 0, 1, way).start()
-    cache_load.start()
+    step1(1, 0, 1, 0).start()
     terms(3)
     add_cores(2)
-    for way in range(2):
-        step1(2, 1, 1, way).start()
-    for one in w_loads:
-        one.start()
-
-    mine = e1_sum[f].astype(F32)
-    for d in range(1, 8):
-        e1b(d).wait_recv()
-        mine = mine + e1b_recv[d].astype(F32)
-    e2[t] = mine.astype(BF16)
+    step1(2, 1, 1, 0).start()
+    add_cores(3)
+    step2_go(0)
+    step1(0, 0, 0, 1).start()
+    step1(0, 1, 0, 1).start()
+    step1(1, 0, 1, 1).start()
+    step1(2, 1, 1, 1).start()
+
+    total = e1_send[gf].astype(F32)
+    for d in range(1, 16):
+        e1(d).wait_recv()
+        total = total + e1_recv[d].astype(F32)
+    e2[t] = total.astype(BF16)
+
+    lined = gf // 2 == t
+
+    def e3(a, b):
+        to_h, to_t = (h + a) % 2, (t + b) % 8
+        return pltpu.make_async_remote_copy(
+            src_ref=e2.at[t, pl.ds(pl.multiple_of(16 * to_h, 16), 4 * PAD)],
+            dst_ref=e3_recv.at[gf],
+            send_sem=e3_sem.at[0, 8 * a + b],
+            recv_sem=e3_sem.at[1, gf],
+            device_id=(t // 4, (t % 4) * 2 + to_h, to_t),
+            device_id_type=MESH,
+        )
+
+    def e3_arrival(d):
+        source = (gf + d) % 16
+        return pltpu.make_async_remote_copy(
+            src_ref=e2.at[t, pl.ds(0, 4 * PAD)],
+            dst_ref=e3_recv.at[source],
+            send_sem=e3_sem.at[0, 0],
+            recv_sem=e3_sem.at[1, source],
+            device_id=gf_peer(1),
+            device_id_type=MESH,
+        )
+
+    for a in range(2):
+        for b in range(8):
+            if a + b:
+                e3(a, b).start()
+
+    @pl.when(jnp.logical_not(lined))
+    def _():
+        e3(0, 0).start()
+
+    @pl.when(lined)
+    def _():
+        e3_recv[gf] = e2[t, pl.ds(pl.multiple_of(16 * h, 16), 4 * PAD), :]
 
     def e2_copy(d):
         return remote(e2.at[t], e2.at[t], e2_sem, (d,), tp_peer(d))
@@ -286,8 +327,14 @@
     for d in range(1, 8):
         e2_copy(d).start()
 
-    add_cores(3)
-    step2_go(0)
+    gain32[...] = gain[...].astype(F32)
+    fresh[...] = jnp.zeros_like(fresh)
+
+    for ab in range(2):
+        send3[ab] = x_sum(ab, 0).astype(BF16)
+        step3(ab).start()
+
+    step2_go(1)
 
     for d in range(1, 8):
         e2_arrival(d).wait_recv()
@@ -295,54 +342,81 @@
     for n in range(8):
         emb = e2[n].astype(F32)
         for b in range(5):
+            k = n * 5 + b
             one = emb[b * PAD : (b + 1) * PAD]
             square = square + one * one
+            scaled[:, k * HEAD : (k + 1) * HEAD] = one * gain32[k : k + 1, :]
     mean = jnp.sum(square, axis=-1, keepdims=True) * (1.0 / WIDTH)
     factor = lax.rsqrt(mean + norm_eps)
-    for n in range(8):
-        emb = e2[n].astype(F32)
-        for b in range(5):
-            k = n * 5 + b
-            one = emb[b * PAD : (b + 1) * PAD] * gain_ref[:, pl.ds(k * HEAD, HEAD)] * factor
-            one = one.astype(BF16).astype(F32)
-            tiles[pl.ds(k * PAD, PAD), :] = one
-            normed[:, pl.ds(k * HEAD, HEAD)] = one
-    tiles[pl.ds(40 * PAD, 2 * PAD), :] = jnp.zeros((2 * PAD, HEAD), F32)
-
-    def e3_block(device):
-        first = (device // 2) * 5 + 2 * (device % 2)
-        return tiles[pl.ds(pl.multiple_of(first * PAD, PAD), 4 * PAD), :].astype(BF16)
-
-    def e3(d):
-        return remote(e3_send.at[d], e3_recv.at[d], e3_sem, (d,), gf_peer(d))
-
-    for d in range(1, 16):
-        e3_send[d] = e3_block((gf + d) % 16)
-        e3(d).start()
-    e3_recv[0] = e3_block(gf)
-
-    step2_go(1)
 
     qw_load.wait()
-    normed16 = normed[...].astype(BF16)
+    scaled16 = scaled[...].astype(BF16)
 
     @pl.loop(0, 4)
     def _(n):
         columns = pl.ds(pl.multiple_of(n * 256, 256), 256)
-        qraw[:, columns] = jnp.dot(normed16, qw[:, columns], preferred_element_type=F32)
-
-    cosine, sine = cos_ref[...], sin_ref[...]
+        qraw[:, columns] = jnp.dot(scaled16, qw[:, columns], preferred_element_type=F32)
+
+    place = lax.broadcasted_iota(jnp.int32, (PAD, HEAD), 0)
+    lane = lax.broadcasted_iota(jnp.int32, (PAD, HEAD), 1)
+    position = jnp.where(place % 2 == 0, len_ref[0], len_ref[1]) + place // 2
+    freqs = jnp.exp((lane % (HEAD // 2)).astype(F32) * (-rope_log * 2.0 / HEAD))
+    angles = position.astype(F32) * freqs
+    cosine, sine = jnp.cos(angles), jnp.sin(angles)
+    sine = jnp.where(lane < HEAD // 2, -sine, sine)
 
     def rotate(values):
         return values * cosine + pltpu.roll(values, HEAD // 2, 1) * sine
 
     query = jnp.concatenate(
-        [rotate(head_norm(qraw[:, g * HEAD : (g + 1) * HEAD])) for g in range(HEADS)], axis=0
+        [
+            rotate(head_norm(qraw[:, g * HEAD : (g + 1) * HEAD] * factor))
+            for g in range(HEADS)
+        ],
+        axis=0,
     ).astype(BF16)
 
+    @pl.when(jnp.logical_not(lined))
+    def _():
+        e3_arrival(0).wait_recv()
+
+    for d in range(1, 16):
+        e3_arrival(d).wait_recv()
+    first = (gf // 2) * 5 + 2 * h
+    arrived = [e3_recv[n].astype(F32) for n in range(16)]
+    features = jnp.concatenate(
+        [
+            jnp.concatenate([one[b * PAD : (b + 1) * PAD] for one in arrived], axis=0)
+            * gain32[pl.ds(first + b, 1), :]
+            for b in range(3)
+        ],
+        axis=1,
+    ).astype(BF16)
+
+    for one in w_loads:
+        one.wait()
     for ab in range(2):
-        send3[ab] = x_sum(ab, 0).astype(BF16)
-        step3(ab).start()
+        total = x_sum(ab, 1)
+        step3(ab).wait_recv()
+        total = total + recv3[ab].astype(F32)
+        every = pl.ds(ab, OWN, 2)
+        grad[every, :] = total
+        new_weight, _, _ = adam(wm[0, every, :], wm[1, every, :], wm[2, every, :], total)
+        fresh[pl.ds(pl.multiple_of(h * 64, 64), OWN), pl.ds(ab * HEAD, HEAD)] = new_weight.astype(
+            BF16
+        )
+    partial = jnp.dot(features, fresh[...], preferred_element_type=F32)
+
+    def kv(d):
+        return remote(kv_send.at[(gf + d) % 16], kv_recv.at[d], kv_sem, (d,), gf_peer(d))
+
+    for n in range(16):
+        rows = partial[n * PAD : (n + 1) * PAD]
+        kv_send[n] = jnp.concatenate([rows[:, :HEAD], rows[:, HEAD:]], axis=0).astype(BF16)
+    for d in range(1, 16):
+        kv(d).start()
+    grad_store = load(grad, grad_hbm, 18)
+    grad_store.start()
 
     scale = 1.0 / math.sqrt(HEAD)
     cache_load.wait()
@@ -375,62 +449,30 @@
             )
         )
     token = lax.broadcasted_iota(jnp.int32, (HEADS * PAD, 1), 0) % PAD
-    first_row = token < STEPS
+    first_row = token % 2 == 0
     denom = jnp.where(first_row, sums[0][0], sums[1][0])
     numer = jnp.where(first_row, sums[0][1], sums[1][1])
 
-    for d in range(1, 16):
-        e3(d).wait_recv()
-    arrived = [e3_recv[d].astype(F32) for d in range(16)]
-    features = jnp.concatenate(
-        [
-            jnp.concatenate([one[b * PAD : (b + 1) * PAD] for one in arrived], axis=0)
-            for b in range(3)
-        ],
-        axis=1,
-    ).astype(BF16)
-
-    fresh[...] = jnp.zeros_like(fresh)
-    for one in w_loads:
-        one.wait()
-    for ab in range(2):
-        total = x_sum(ab, 1)
-        step3(ab).wait_recv()
-        total = total + recv3[ab].astype(F32)
-        every = pl.ds(ab, OWN, 2)
-        grad_ref[every, :] = total
-        new_weight, _, _ = adam(wm[0, every, :], wm[1, every, :], wm[2, every, :], total)
-        fresh[pl.ds(pl.multiple_of(h * 64, 64), OWN), pl.ds(ab * HEAD, HEAD)] = new_weight.astype(
-            BF16
-        )
-    partial = jnp.dot(features, fresh[...], preferred_element_type=F32)
-
-    def kv(d):
-        return remote(kv_send.at[d], kv_recv.at[d], kv_sem, (d,), gf_peer(16 - d))
-
-    for d in range(1, 16):
-        rows = partial[d * PAD : (d + 1) * PAD]
-        kv_send[d] = jnp.concatenate([rows[:, :HEAD], rows[:, HEAD:]], axis=0).astype(BF16)
-        kv(d).start()
-    total = jnp.concatenate([partial[:PAD, :HEAD], partial[:PAD, HEAD:]], axis=0)
+    total = kv_send[gf].astype(F32)
     for d in range(1, 16):
         kv(d).wait_recv()
         total = total + kv_recv[d].astype(F32)
-    new_key = rotate(head_norm(total[:PAD])).astype(BF16).astype(F32)
-    new_value = total[PAD:].astype(BF16).astype(F32)
+    new_key = rotate(head_norm(total[:PAD] * factor)).astype(BF16).astype(F32)
+    new_value = (total[PAD:] * factor).astype(BF16).astype(F32)
     kv_ref[0] = new_key
     kv_ref[1] = new_value
 
     query32 = query.astype(F32)
     for j in range(2 * STEPS):
         score = jnp.sum(query32 * new_key[j : j + 1], axis=-1, keepdims=True) * scale
-        seen = (token // STEPS == j // STEPS) & (token >= j)
+        seen = (token % 2 == j % 2) & (token >= j)
         weight = jnp.where(seen, jnp.exp(score), 0.0)
         denom = denom + weight
         numer = numer + weight.astype(BF16).astype(F32) * new_value[j : j + 1]
     attended = numer / denom
     for g in range(HEADS):
         att_ref[:, pl.ds(g * HEAD, HEAD)] = attended[g * PAD : (g + 1) * PAD]
+    grad_store.wait()
 
     for i in range(4):
         core_copy(i).wait_send()
@@ -441,13 +483,28 @@
             step2(ab, way).wait_send()
     for ab in range(2):
         step3(ab).wait_send()
-    e1a.wait_send()
     for d in range(1, 8):
-        e1b(d).wait_send()
         e2_copy(d).wait_send()
     for d in range(1, 16):
-        e3(d).wait_send()
+        e1(d).wait_send()
         kv(d).wait_send()
+    for a in range(2):
+        for b in range(8):
+            if a + b:
+                e3(a, b).wait_send()
+
+    @pl.when(jnp.logical_not(lined))
+    def _():
+        e3(0, 0).wait_send()
+
+
+def finish(w_ref, m_ref, v_ref, grad_ref, kv_ref, att_ref, nw_ref, nm_ref, nv_ref, nkv_ref, out_ref):
+    nw_ref[...], nm_ref[...], nv_ref[...] = adam(w_ref[...], m_ref[...], v_ref[...], grad_ref[...])
+    for s in range(STEPS):
+        rows = slice(2 * s, 2 * s + 2)
+        out_ref[s] = att_ref[rows, :].astype(BF16)
+        for n in range(2):
+            nkv_ref[n, s] = kv_ref[n, rows, :].astype(BF16)
 
 
 def shards(
@@ -464,22 +521,9 @@
     lengths,
 ):
     rows = lengths.shape[0]
-    tokens = rows * STEPS
-
-    ids = jnp.pad(token_ids.reshape(16, tokens), ((0, 0), (0, PAD - tokens)), constant_values=-1)
-    ids = ids.reshape(16 * PAD, 1)
-    positions = (lengths[:, None] + jnp.arange(STEPS, dtype=jnp.int32)[None, :]).reshape(tokens, 1)
-    half = HEAD // 2
-    freqs = jnp.exp(-rope_log * 2.0 * jnp.arange(half, dtype=F32) / HEAD)
-    angles = positions.astype(F32) * freqs
-    angles = jnp.pad(angles, ((0, PAD - tokens), (0, 0)))
-    cosine, sine = jnp.cos(angles), jnp.sin(angles)
-    cosine = jnp.concatenate([cosine, cosine], axis=1)
-    sine = jnp.concatenate([-sine, sine], axis=1)
-
+    state = [one.reshape(2 * OWN, HEAD) for one in (weight, moment, second)]
     anywhere = pl.BlockSpec(memory_space=pl.ANY)
     vmem = pl.BlockSpec(memory_space=pltpu.VMEM)
-    smem = pl.BlockSpec(memory_space=pltpu.SMEM)
     dma = pltpu.SemaphoreType.DMA
     grad, kv, att = pl.pallas_call(
         kernel,
@@ -488,8 +532,8 @@
             jax.ShapeDtypeStruct((2, PAD, HEAD), F32),
             jax.ShapeDtypeStruct((PAD, HEADS * HEAD), F32),
         ),
-        in_specs=[anywhere] * 6 + [vmem] + [anywhere] * 2 + [vmem] * 3 + [smem],
-        out_specs=(vmem, vmem, vmem),
+        in_specs=[anywhere] * 11,
+        out_specs=(anywhere, vmem, vmem),
         scratch_shapes=[
             pltpu.VMEM((8, TOK, CHUNK), BF16),
             pltpu.VMEM((2 * TOK, HEAD), BF16),
@@ -508,26 +552,26 @@
             pltpu.VMEM((2, 2, OWN, HEAD), BF16),
             pltpu.VMEM((2, OWN, HEAD), BF16),
             pltpu.VMEM((2, OWN, HEAD), BF16),
-            pltpu.VMEM((2, 8, 6 * PAD, HEAD), BF16),
+            pltpu.VMEM((16, 6 * PAD, HEAD), BF16),
+            pltpu.VMEM((16, 6 * PAD, HEAD), BF16),
             pltpu.VMEM((8, 6 * PAD, HEAD), BF16),
-            pltpu.VMEM((8, 6 * PAD, HEAD), BF16),
-            pltpu.VMEM((8, 6 * PAD, HEAD), BF16),
-            pltpu.VMEM((8, 6 * PAD, HEAD), BF16),
-            pltpu.VMEM((42 * PAD, HEAD), F32),
             pltpu.VMEM((PAD, WIDTH), F32),
             pltpu.VMEM((PAD, HEADS * HEAD), F32),
-            pltpu.VMEM((16, 4 * PAD, HEAD), BF16),
             pltpu.VMEM((16, 4 * PAD, HEAD), BF16),
             pltpu.VMEM((3 * HEAD, 2 * HEAD), BF16),
             pltpu.VMEM((16, 2 * PAD, HEAD), BF16),
             pltpu.VMEM((16, 2 * PAD, HEAD), BF16),
-            dma((15,)),
+            pltpu.VMEM((WIDTH // HEAD, HEAD), BF16),
+            pltpu.VMEM((WIDTH // HEAD, HEAD), F32),
+            pltpu.VMEM((STEPS, 32), jnp.int32),
+            pltpu.SMEM((2,), jnp.int32),
+            pltpu.VMEM((2 * OWN, HEAD), F32),
+            dma((19,)),
             dma((2, 4)),
             dma((2, 2, 2, 2)),
             dma((2, 2, 2)),
             dma((2, 2)),
-            dma((2,)),
-            dma((2, 8)),
+            dma((2, 16)),
             dma((2, 8)),
             dma((2, 16)),
             dma((2, 16)),
@@ -539,23 +583,31 @@
     )(
         learn_input,
         learn_cotangent.reshape(2 * TOK, HEAD),
-        weight.reshape(2 * OWN, HEAD),
-        moment.reshape(2 * OWN, HEAD),
-        second.reshape(2 * OWN, HEAD),
+        *state,
         table,
-        gain.astype(F32).reshape(1, WIDTH),
+        gain.reshape(WIDTH // HEAD, HEAD),
         query_weight,
         cache.reshape(2, rows, POSITIONS, HEAD),
-        ids,
-        cosine,
-        sine,
+        token_ids.T,
         lengths,
     )
-    new_weight, new_moment, new_second = adam(
-        weight, moment, second, grad.reshape(OWN, 2, HEAD)
-    )
-    new_kv = kv[:, :tokens].reshape(2, rows, 1, STEPS, HEAD).astype(BF16)
-    attended = att[:tokens].reshape(rows, STEPS, HEADS * HEAD).astype(BF16)
+    like = jax.ShapeDtypeStruct((2 * OWN, HEAD), F32)
+    *updated, new_kv, attended = pl.pallas_call(
+        finish,
+        out_shape=(
+            like,
+            like,
+            like,
+            jax.ShapeDtypeStruct((2, STEPS, 2, HEAD), BF16),
+            jax.ShapeDtypeStruct((STEPS, 2, HEADS * HEAD), BF16),
+        ),
+        in_specs=[vmem] * 6,
+        out_specs=(vmem,) * 5,
+        name="finish",
+    )(*state, grad, kv, att)
+    new_weight, new_moment, new_second = (one.reshape(OWN, 2, HEAD) for one in updated)
+    new_kv = new_kv.transpose(0, 2, 1, 3).reshape(2, rows, 1, STEPS, HEAD)
+    attended = attended.transpose(1, 0, 2)
     return new_weight, new_moment, new_second, new_kv, attended
 
 

time: 51.5 us -> 41.7 us (0.81)
  other arithmetic: 5.82 us -> 0 us
  local copies, waits for them, and re-layouts: 4.33 us -> 0 us
    sub x1 -> x0, other arithmetic: 2.97 us -> none  [adam(): new_weight = weight - learn_rate * (update + weight_decay * weight)]
    pallas_call x0 -> x1, Pallas kernels: none -> 2.45 us  [shards(): pl.pallas_call(finish, out_shape=(like, like, like, jax.ShapeDtypeStruct(...]
    unnamed x9 -> x0, local copies, waits for them, and re-layouts: 1.97 us -> none
    pallas_call x1, Pallas kernels: 40.4 us -> 38.4 us  [shards(): pl.pallas_call(kernel, out_shape=(jax.ShapeDtypeStruct((2 * OWN, HEAD), F...]
    slice x3 -> x0, local copies, waits for them, and re-layouts: 1.47 us -> none  [the longest x1 0.76 us: shards(): attended = att[:tokens].reshape(rows, STEPS, HEADS * HEAD).astype(BF16)]
    reshape x1 -> x0, other arithmetic: 1.31 us -> none  [shards(): gain.astype(F32).reshape(1, WIDTH)]
    reshape x2 -> x0, local copies, waits for them, and re-layouts: 0.78 us -> none  [the longest x1 0.71 us: shards(): ids = ids.reshape(16 * PAD, 1)]
    convert_element_type x1 -> x0, other arithmetic: 0.73 us -> none  [shards(): angles = positions.astype(F32) * freqs]
where the time goes in v2:
time: 41.7 us; the launch traced here: 41.5 us
  Pallas kernels  40.9 us (98%)
  between operations  0.64 us (2%)
    pallas_call x1, Pallas kernels, shards(): pl.pallas_call(kernel, out_shape=(jax.ShapeDtypeStruct((2 * OWN, HEAD), F...  38.4 us
    pallas_call x1, Pallas kernels, shards(): pl.pallas_call(finish, out_shape=(like, like, like, jax.ShapeDtypeStruct(...  2.45 us

profile of v2, /device:TPU:1, one launch (start us, length us, event | category | flops | bytes accessed | tf_op | source)
XLA Modules:
  0.0 41.5 jit_solution(17689719875952233060)
XLA Ops:
  0.6 38.4 %step.1 = (f32[640,128]{1,0:T(8,128)}, f32[2,8,128]{2,1,0:T(8,128)}, f32[8,1024]{1,0:T(8,128)}) custom-call(bf16[1024,5120]{1,0:T(8,128)(2,1)} %li_hbm.1, bf16[2048,128]{1,0:T(8,128)(2,1)} %bitcast.23, f32[640,128]{1,0:T(8,128)} %bitcast.17, f32[640,128]{1,0:T(8,128)} %bitcast.19, f32[640,128]{1,0:T(8,128)} %bitcast.21, bf16[4864,640]{1,0:T(8,128)(2,1)} %table_hbm.1, ...), custom_call_target="tpu_custom_call" | custom-call | tf_op jit(solution)/shard_map/step/pallas_call | solution.py:528
  39.1 2.4 %finish.1 = (f32[640,128]{1,0:T(8,128)}, f32[640,128]{1,0:T(8,128)}, f32[640,128]{1,0:T(8,128)}, bf16[2,3,2,128]{3,2,1,0:T(2,128)(2,1)}, bf16[3,2,1024]{2,1,0:T(2,128)(2,1)}) custom-call(f32[640,128]{1,0:T(8,128)} %bitcast.18, f32[640,128]{1,0:T(8,128)} %bitcast.20, f32[640,128]{1,0:T(8,128)} %bitcast.22, f32[640,128]{1,0:T(8,128)} %get-tuple-element.13.grad_ref, ...), custom_call_target="tpu_custom_call" | custom-call | tf_op jit(solution)/shard_map/finish/pallas_call | solution.py:595

commit v3 on v2

--- a/solution.py
+++ b/solution.py
@@ -1,4 +1,3 @@
-import functools
 import math
 
 import jax
@@ -81,8 +80,10 @@
     e1_send,
     e1_recv,
     e2,
+    tiles,
     scaled,
     qraw,
+    e3_send,
     e3_recv,
     fresh,
     kv_send,
@@ -268,73 +269,36 @@
     add_cores(2)
     step1(2, 1, 1, 0).start()
     add_cores(3)
+
+    total = e1_send[gf].astype(F32)
+    for d in range(1, 16):
+        e1(d).wait_recv()
+        total = total + e1_recv[d].astype(F32)
+    e2[t] = total.astype(BF16)
+
+    def e2_copy(d):
+        return remote(e2.at[t], e2.at[t], e2_sem, (d,), tp_peer(d))
+
+    def e2_arrival(d):
+        there = (t + 8 - d) % 8
+        return remote(e2.at[there], e2.at[there], e2_sem, (d,), tp_peer(d))
+
+    for d in range(1, 8):
+        e2_copy(d).start()
+
     step2_go(0)
     step1(0, 0, 0, 1).start()
     step1(0, 1, 0, 1).start()
     step1(1, 0, 1, 1).start()
     step1(2, 1, 1, 1).start()
 
-    total = e1_send[gf].astype(F32)
-    for d in range(1, 16):
-        e1(d).wait_recv()
-        total = total + e1_recv[d].astype(F32)
-    e2[t] = total.astype(BF16)
-
-    lined = gf // 2 == t
-
-    def e3(a, b):
-        to_h, to_t = (h + a) % 2, (t + b) % 8
-        return pltpu.make_async_remote_copy(
-            src_ref=e2.at[t, pl.ds(pl.multiple_of(16 * to_h, 16), 4 * PAD)],
-            dst_ref=e3_recv.at[gf],
-            send_sem=e3_sem.at[0, 8 * a + b],
-            recv_sem=e3_sem.at[1, gf],
-            device_id=(t // 4, (t % 4) * 2 + to_h, to_t),
-            device_id_type=MESH,
-        )
-
-    def e3_arrival(d):
-        source = (gf + d) % 16
-        return pltpu.make_async_remote_copy(
-            src_ref=e2.at[t, pl.ds(0, 4 * PAD)],
-            dst_ref=e3_recv.at[source],
-            send_sem=e3_sem.at[0, 0],
-            recv_sem=e3_sem.at[1, source],
-            device_id=gf_peer(1),
-            device_id_type=MESH,
-        )
-
-    for a in range(2):
-        for b in range(8):
-            if a + b:
-                e3(a, b).start()
-
-    @pl.when(jnp.logical_not(lined))
-    def _():
-        e3(0, 0).start()
-
-    @pl.when(lined)
-    def _():
-        e3_recv[gf] = e2[t, pl.ds(pl.multiple_of(16 * h, 16), 4 * PAD), :]
-
-    def e2_copy(d):
-        return remote(e2.at[t], e2.at[t], e2_sem, (d,), tp_peer(d))
-
-    def e2_arrival(d):
-        there = (t + 8 - d) % 8
-        return remote(e2.at[there], e2.at[there], e2_sem, (d,), tp_peer(d))
-
-    for d in range(1, 8):
-        e2_copy(d).start()
-
     gain32[...] = gain[...].astype(F32)
     fresh[...] = jnp.zeros_like(fresh)
+    tiles[pl.ds(40 * PAD, 2 * PAD), :] = jnp.zeros((2 * PAD, HEAD), F32)
 
     for ab in range(2):
         send3[ab] = x_sum(ab, 0).astype(BF16)
         step3(ab).start()
-
-    step2_go(1)
 
     for d in range(1, 8):
         e2_arrival(d).wait_recv()
@@ -342,12 +306,37 @@
     for n in range(8):
         emb = e2[n].astype(F32)
         for b in range(5):
-            k = n * 5 + b
             one = emb[b * PAD : (b + 1) * PAD]
             square = square + one * one
-            scaled[:, k * HEAD : (k + 1) * HEAD] = one * gain32[k : k + 1, :]
     mean = jnp.sum(square, axis=-1, keepdims=True) * (1.0 / WIDTH)
     factor = lax.rsqrt(mean + norm_eps)
+    for n in range(8):
+        emb = e2[n].astype(F32)
+        for b in range(5):
+            k = n * 5 + b
+            one = emb[b * PAD : (b + 1) * PAD] * gain32[k : k + 1, :] * factor
+            tiles[pl.ds(k * PAD, PAD), :] = one
+            scaled[:, k * HEAD : (k + 1) * HEAD] = one
+
+    def e3_block(device):
+        first = (device // 2) * 5 + 2 * (device % 2)
+        return tiles[pl.ds(pl.multiple_of(first * PAD, PAD), 4 * PAD), :].astype(BF16)
+
+    for n in range(16):
+        e3_send[n] = e3_block(n)
+
+    def e3(d):
+        return remote(e3_send.at[(gf + d) % 16], e3_recv.at[gf], e3_sem, (d,), gf_peer(d))
+
+    def e3_arrival(d):
+        there = (gf + 16 - d) % 16
+        return remote(e3_send.at[there], e3_recv.at[there], e3_sem, (d,), gf_peer(d))
+
+    for d in range(1, 16):
+        e3(d).start()
+    e3_recv[gf] = e3_send[gf]
+
+    step2_go(1)
 
     qw_load.wait()
     scaled16 = scaled[...].astype(BF16)
@@ -370,24 +359,18 @@
 
     query = jnp.concatenate(
         [
-            rotate(head_norm(qraw[:, g * HEAD : (g + 1) * HEAD] * factor))
+            rotate(head_norm(qraw[:, g * HEAD : (g + 1) * HEAD]))
             for g in range(HEADS)
         ],
         axis=0,
     ).astype(BF16)
 
-    @pl.when(jnp.logical_not(lined))
-    def _():
-        e3_arrival(0).wait_recv()
-
     for d in range(1, 16):
         e3_arrival(d).wait_recv()
-    first = (gf // 2) * 5 + 2 * h
     arrived = [e3_recv[n].astype(F32) for n in range(16)]
     features = jnp.concatenate(
         [
             jnp.concatenate([one[b * PAD : (b + 1) * PAD] for one in arrived], axis=0)
-            * gain32[pl.ds(first + b, 1), :]
             for b in range(3)
         ],
         axis=1,
@@ -457,8 +440,8 @@
     for d in range(1, 16):
         kv(d).wait_recv()
         total = total + kv_recv[d].astype(F32)
-    new_key = rotate(head_norm(total[:PAD] * factor)).astype(BF16).astype(F32)
-    new_value = (total[PAD:] * factor).astype(BF16).astype(F32)
+    new_key = rotate(head_norm(total[:PAD])).astype(BF16).astype(F32)
+    new_value = total[PAD:].astype(BF16).astype(F32)
     kv_ref[0] = new_key
     kv_ref[1] = new_value
 
@@ -487,15 +470,8 @@
         e2_copy(d).wait_send()
     for d in range(1, 16):
         e1(d).wait_send()
+        e3(d).wait_send()
         kv(d).wait_send()
-    for a in range(2):
-        for b in range(8):
-            if a + b:
-                e3(a, b).wait_send()
-
-    @pl.when(jnp.logical_not(lined))
-    def _():
-        e3(0, 0).wait_send()
 
 
 def finish(w_ref, m_ref, v_ref, grad_ref, kv_ref, att_ref, nw_ref, nm_ref, nv_ref, nkv_ref, out_ref):
@@ -555,8 +531,10 @@
             pltpu.VMEM((16, 6 * PAD, HEAD), BF16),
             pltpu.VMEM((16, 6 * PAD, HEAD), BF16),
             pltpu.VMEM((8, 6 * PAD, HEAD), BF16),
+            pltpu.VMEM((42 * PAD, HEAD), F32),
             pltpu.VMEM((PAD, WIDTH), F32),
             pltpu.VMEM((PAD, HEADS * HEAD), F32),
+            pltpu.VMEM((16, 4 * PAD, HEAD), BF16),
             pltpu.VMEM((16, 4 * PAD, HEAD), BF16),
             pltpu.VMEM((3 * HEAD, 2 * HEAD), BF16),
             pltpu.VMEM((16, 2 * PAD, HEAD), BF16),

time: 41.7 us -> 36.4 us (0.87)
  Pallas kernels: 40.9 us -> 35.7 us
    pallas_call x1, Pallas kernels: 38.4 us -> 33.2 us  [shards(): pl.pallas_call(kernel, out_shape=(jax.ShapeDtypeStruct((2 * OWN, HEAD), F...]
where the time goes in v3:
time: 36.4 us; the launch traced here: 36.3 us
  Pallas kernels  35.7 us (98%)
  between operations  0.64 us (2%)
    pallas_call x1, Pallas kernels, shards(): pl.pallas_call(kernel, out_shape=(jax.ShapeDtypeStruct((2 * OWN, HEAD), F...  33.2 us
    pallas_call x1, Pallas kernels, shards(): pl.pallas_call(finish, out_shape=(like, like, like, jax.ShapeDtypeStruct(...  2.45 us

profile of v3, /device:TPU:1, one launch (start us, length us, event | category | flops | bytes accessed | tf_op | source)
XLA Modules:
  0.0 36.3 jit_solution(12220096327440714794)
XLA Ops:
  0.6 33.2 %step.1 = (f32[640,128]{1,0:T(8,128)}, f32[2,8,128]{2,1,0:T(8,128)}, f32[8,1024]{1,0:T(8,128)}) custom-call(bf16[1024,5120]{1,0:T(8,128)(2,1)} %li_hbm.1, bf16[2048,128]{1,0:T(8,128)(2,1)} %bitcast.23, f32[640,128]{1,0:T(8,128)} %bitcast.17, f32[640,128]{1,0:T(8,128)} %bitcast.19, f32[640,128]{1,0:T(8,128)} %bitcast.21, bf16[4864,640]{1,0:T(8,128)(2,1)} %table_hbm.1, ...), custom_call_target="tpu_custom_call" | custom-call | tf_op jit(solution)/shard_map/step/pallas_call | solution.py:504
  33.9 2.4 %finish.1 = (f32[640,128]{1,0:T(8,128)}, f32[640,128]{1,0:T(8,128)}, f32[640,128]{1,0:T(8,128)}, bf16[2,3,2,128]{3,2,1,0:T(2,128)(2,1)}, bf16[3,2,1024]{2,1,0:T(2,128)(2,1)}) custom-call(f32[640,128]{1,0:T(8,128)} %bitcast.18, f32[640,128]{1,0:T(8,128)} %bitcast.20, f32[640,128]{1,0:T(8,128)} %bitcast.22, f32[640,128]{1,0:T(8,128)} %get-tuple-element.13.grad_ref, ...), custom_call_target="tpu_custom_call" | custom-call | tf_op jit(solution)/shard_map/finish/pallas_call | solution.py:573

commit v4 on v3

--- a/solution.py
+++ b/solution.py
@@ -20,7 +20,9 @@
 POSITIONS = 4096
 OWN = 320
 CHUNK = 640
+TOKENS = 6
 PAD = 8
+ROWS = 32
 
 learn_rate = 0.002
 beta_one = 0.9
@@ -57,7 +59,9 @@
     cache_hbm,
     ids_hbm,
     len_hbm,
-    grad_hbm,
+    nw_hbm,
+    nm_hbm,
+    nv_hbm,
     kv_ref,
     att_ref,
     li,
@@ -77,14 +81,15 @@
     recv2,
     send3,
     recv3,
+    e1_pack,
     e1_send,
     e1_recv,
     e2,
-    tiles,
+    e2_wide,
     scaled,
     qraw,
-    e3_send,
     e3_recv,
+    e3_wide,
     fresh,
     kv_send,
     kv_recv,
@@ -92,7 +97,7 @@
     gain32,
     ids,
     len_ref,
-    grad,
+    updated,
     load_sem,
     core_sem,
     s1_sem,
@@ -143,7 +148,11 @@
         return load(li_hbm.at[:, pl.ds(column, CHUNK)], li.at[j], j)
 
     cot_load = load(cot_hbm, cot, 8)
-    table_load = load(table_hbm, table, 9)
+    part_rows = VOCAB_OWN // 2
+    table_parts = [pl.ds(n * part_rows, part_rows) for n in range(2)]
+    table_loads = [
+        load(table_hbm.at[rows], table.at[rows], n) for rows, n in zip(table_parts, (9, 21))
+    ]
     w_loads = [load(ref, wm.at[n], 10 + n) for n, ref in enumerate((w_hbm, m_hbm, v_hbm))]
     qw_load = load(qw_hbm, qw, 13)
     cache_load = load(cache_hbm, cache, 14)
@@ -153,7 +162,8 @@
     cot_load.start()
     for one in small_loads:
         one.start()
-    table_load.start()
+    for one in table_loads:
+        one.start()
     for j in range(8):
         li_load(j).start()
 
@@ -241,14 +251,20 @@
     hot = jnp.where(
         lax.broadcasted_iota(jnp.int32, (16 * PAD, VOCAB_OWN), 1) == wanted - gf * VOCAB_OWN, 1.0, 0.0
     ).astype(BF16)
-    table_load.wait()
-    picked = jnp.dot(hot, table[...], preferred_element_type=F32)
-    blank = jnp.zeros((PAD, HEAD), F32)
+    picked = jnp.zeros((16 * PAD, CHUNK), F32)
+    for n in range(2):
+        table_loads[n].wait()
+        columns = slice(n * part_rows, (n + 1) * part_rows)
+        picked = picked + jnp.dot(
+            hot[:, columns], table[table_parts[n], :], preferred_element_type=F32
+        )
+    e1_pack[...] = jnp.zeros_like(e1_pack)
     for device in range(16):
-        rows = picked[device * PAD : (device + 1) * PAD]
-        e1_send[device] = jnp.concatenate(
-            [rows[:, b * HEAD : (b + 1) * HEAD] for b in range(5)] + [blank], axis=0
-        ).astype(BF16)
+        for b in range(5):
+            e1_pack[device, b * TOKENS : (b + 1) * TOKENS, :] = picked[
+                device * PAD : device * PAD + TOKENS, b * HEAD : (b + 1) * HEAD
+            ]
+    e1_send[...] = e1_pack[...].astype(BF16)
 
     def e1(d):
         return remote(e1_send.at[(gf + d) % 16], e1_recv.at[d], e1_sem, (d,), gf_peer(d))
@@ -286,57 +302,72 @@
     for d in range(1, 8):
         e2_copy(d).start()
 
+    def e3(d, a):
+        source = (t + 8 - d) % 8
+        to = 2 * source + (h + a) % 2
+        return pltpu.make_async_remote_copy(
+            src_ref=e2.at[source],
+            dst_ref=e3_recv.at[gf],
+            send_sem=e3_sem.at[0, 2 * d + a],
+            recv_sem=e3_sem.at[1, gf],
+            device_id=(to // 8, to % 8, t),
+            device_id_type=MESH,
+        )
+
+    def e3_arrival(d):
+        there = (gf + d) % 16
+        return pltpu.make_async_remote_copy(
+            src_ref=e2.at[0],
+            dst_ref=e3_recv.at[there],
+            send_sem=e3_sem.at[0, 0],
+            recv_sem=e3_sem.at[1, there],
+            device_id=gf_peer(d),
+            device_id_type=MESH,
+        )
+
+    def itself(d):
+        return (t + 8 - d) % 8 == gf // 2
+
+    def e3_go(d):
+        e3(d, 1).start()
+
+        @pl.when(jnp.logical_not(itself(d)))
+        def _():
+            e3(d, 0).start()
+
+        @pl.when(itself(d))
+        def _():
+            e3_recv[gf] = e2[gf // 2]
+
+    e3_go(0)
     step2_go(0)
     step1(0, 0, 0, 1).start()
     step1(0, 1, 0, 1).start()
     step1(1, 0, 1, 1).start()
     step1(2, 1, 1, 1).start()
-
     gain32[...] = gain[...].astype(F32)
     fresh[...] = jnp.zeros_like(fresh)
-    tiles[pl.ds(40 * PAD, 2 * PAD), :] = jnp.zeros((2 * PAD, HEAD), F32)
-
     for ab in range(2):
         send3[ab] = x_sum(ab, 0).astype(BF16)
         step3(ab).start()
-
-    for d in range(1, 8):
+    for d in (1, 7, 2, 6, 3, 5, 4):
         e2_arrival(d).wait_recv()
+        e3_go(d)
+    step2_go(1)
+    for n in range(8):
+        e2_wide[n] = e2[n].astype(F32)
     square = jnp.zeros((PAD, HEAD), F32)
     for n in range(8):
-        emb = e2[n].astype(F32)
         for b in range(5):
-            one = emb[b * PAD : (b + 1) * PAD]
+            one = e2_wide[n, pl.ds(b * TOKENS, PAD), :]
             square = square + one * one
     mean = jnp.sum(square, axis=-1, keepdims=True) * (1.0 / WIDTH)
     factor = lax.rsqrt(mean + norm_eps)
     for n in range(8):
-        emb = e2[n].astype(F32)
         for b in range(5):
             k = n * 5 + b
-            one = emb[b * PAD : (b + 1) * PAD] * gain32[k : k + 1, :] * factor
-            tiles[pl.ds(k * PAD, PAD), :] = one
+            one = e2_wide[n, pl.ds(b * TOKENS, PAD), :] * gain32[k : k + 1, :] * factor
             scaled[:, k * HEAD : (k + 1) * HEAD] = one
-
-    def e3_block(device):
-        first = (device // 2) * 5 + 2 * (device % 2)
-        return tiles[pl.ds(pl.multiple_of(first * PAD, PAD), 4 * PAD), :].astype(BF16)
-
-    for n in range(16):
-        e3_send[n] = e3_block(n)
-
-    def e3(d):
-        return remote(e3_send.at[(gf + d) % 16], e3_recv.at[gf], e3_sem, (d,), gf_peer(d))
-
-    def e3_arrival(d):
-        there = (gf + 16 - d) % 16
-        return remote(e3_send.at[there], e3_recv.at[there], e3_sem, (d,), gf_peer(d))
-
-    for d in range(1, 16):
-        e3(d).start()
-    e3_recv[gf] = e3_send[gf]
-
-    step2_go(1)
 
     qw_load.wait()
     scaled16 = scaled[...].astype(BF16)
@@ -365,50 +396,13 @@
         axis=0,
     ).astype(BF16)
 
-    for d in range(1, 16):
-        e3_arrival(d).wait_recv()
-    arrived = [e3_recv[n].astype(F32) for n in range(16)]
-    features = jnp.concatenate(
-        [
-            jnp.concatenate([one[b * PAD : (b + 1) * PAD] for one in arrived], axis=0)
-            for b in range(3)
-        ],
-        axis=1,
-    ).astype(BF16)
-
-    for one in w_loads:
-        one.wait()
-    for ab in range(2):
-        total = x_sum(ab, 1)
-        step3(ab).wait_recv()
-        total = total + recv3[ab].astype(F32)
-        every = pl.ds(ab, OWN, 2)
-        grad[every, :] = total
-        new_weight, _, _ = adam(wm[0, every, :], wm[1, every, :], wm[2, every, :], total)
-        fresh[pl.ds(pl.multiple_of(h * 64, 64), OWN), pl.ds(ab * HEAD, HEAD)] = new_weight.astype(
-            BF16
-        )
-    partial = jnp.dot(features, fresh[...], preferred_element_type=F32)
-
-    def kv(d):
-        return remote(kv_send.at[(gf + d) % 16], kv_recv.at[d], kv_sem, (d,), gf_peer(d))
-
-    for n in range(16):
-        rows = partial[n * PAD : (n + 1) * PAD]
-        kv_send[n] = jnp.concatenate([rows[:, :HEAD], rows[:, HEAD:]], axis=0).astype(BF16)
-    for d in range(1, 16):
-        kv(d).start()
-    grad_store = load(grad, grad_hbm, 18)
-    grad_store.start()
-
     scale = 1.0 / math.sqrt(HEAD)
-    cache_load.wait()
     block = 1024
-    sums = []
-    for r in range(2):
+
+    def attend(r):
         length = len_ref[r]
 
-        def attend(n, carry, r=r, length=length):
+        def step(n, carry):
             denom, numer = carry
             where = pl.ds(pl.multiple_of(n * block, block), block)
             scores = lax.dot_general(
@@ -423,25 +417,73 @@
             return denom, numer
 
         rows = HEADS * PAD
-        sums.append(
-            lax.fori_loop(
-                0,
-                POSITIONS // block,
-                attend,
-                (jnp.zeros((rows, 1), F32), jnp.zeros((rows, HEAD), F32)),
+        return lax.fori_loop(
+            0,
+            POSITIONS // block,
+            step,
+            (jnp.zeros((rows, 1), F32), jnp.zeros((rows, HEAD), F32)),
+        )
+
+    cache_load.wait()
+    first_sums = attend(0)
+
+    for d in range(1, 16):
+        e3_arrival(d).wait_recv()
+    e3_wide[...] = e3_recv[...].astype(F32)
+    first = (gf // 2) * 5 + 2 * h
+    columns = []
+    for b in range(3):
+        low, high = [
+            jnp.concatenate(
+                [e3_wide[n, pl.ds((b + start) * TOKENS, PAD), :] for n in range(16)], axis=0
             )
-        )
+            for start in (0, 2)
+        ]
+        columns.append(jnp.where(h == 0, low, high) * gain32[pl.ds(first + b, 1), :])
+    features = jnp.concatenate(columns, axis=1).astype(BF16)
+
+    for one in w_loads:
+        one.wait()
+    for ab in range(2):
+        total = x_sum(ab, 1)
+        step3(ab).wait_recv()
+        total = total + recv3[ab].astype(F32)
+        every = pl.ds(ab, OWN, 2)
+        new_weight, new_moment, new_second = adam(
+            wm[0, every, :], wm[1, every, :], wm[2, every, :], total
+        )
+        updated[0, every, :] = new_weight
+        updated[1, every, :] = new_moment
+        updated[2, every, :] = new_second
+        fresh[pl.ds(pl.multiple_of(h * 64, 64), OWN), pl.ds(ab * HEAD, HEAD)] = new_weight.astype(
+            BF16
+        )
+    partial = jnp.dot(features, fresh[...], preferred_element_type=F32)
+
+    def kv(d):
+        return remote(kv_send.at[(gf + d) % 16], kv_recv.at[d], kv_sem, (d,), gf_peer(d))
+
+    for n in range(16):
+        rows = partial[n * PAD : (n + 1) * PAD]
+        kv_send[n] = jnp.concatenate([rows[:, :HEAD], rows[:, HEAD:]], axis=0).astype(BF16)
+    for d in range(1, 16):
+        kv(d).start()
+    stores = [load(updated.at[n], ref, 18 + n) for n, ref in enumerate((nw_hbm, nm_hbm, nv_hbm))]
+    for one in stores:
+        one.start()
+
+    second_sums = attend(1)
     token = lax.broadcasted_iota(jnp.int32, (HEADS * PAD, 1), 0) % PAD
     first_row = token % 2 == 0
-    denom = jnp.where(first_row, sums[0][0], sums[1][0])
-    numer = jnp.where(first_row, sums[0][1], sums[1][1])
+    denom = jnp.where(first_row, first_sums[0], second_sums[0])
+    numer = jnp.where(first_row, first_sums[1], second_sums[1])
 
     total = kv_send[gf].astype(F32)
     for d in range(1, 16):
         kv(d).wait_recv()
         total = total + kv_recv[d].astype(F32)
-    new_key = rotate(head_norm(total[:PAD])).astype(BF16).astype(F32)
-    new_value = total[PAD:].astype(BF16).astype(F32)
+    new_key = rotate(head_norm(total[:PAD] * factor)).astype(BF16).astype(F32)
+    new_value = (total[PAD:] * factor).astype(BF16).astype(F32)
     kv_ref[0] = new_key
     kv_ref[1] = new_value
 
@@ -455,7 +497,8 @@
     attended = numer / denom
     for g in range(HEADS):
         att_ref[:, pl.ds(g * HEAD, HEAD)] = attended[g * PAD : (g + 1) * PAD]
-    grad_store.wait()
+    for one in stores:
+        one.wait()
 
     for i in range(4):
         core_copy(i).wait_send()
@@ -470,17 +513,39 @@
         e2_copy(d).wait_send()
     for d in range(1, 16):
         e1(d).wait_send()
-        e3(d).wait_send()
         kv(d).wait_send()
-
-
-def finish(w_ref, m_ref, v_ref, grad_ref, kv_ref, att_ref, nw_ref, nm_ref, nv_ref, nkv_ref, out_ref):
-    nw_ref[...], nm_ref[...], nv_ref[...] = adam(w_ref[...], m_ref[...], v_ref[...], grad_ref[...])
+    for d in range(8):
+        e3(d, 1).wait_send()
+
+        @pl.when(jnp.logical_not(itself(d)))
+        def _(d=d):
+            e3(d, 0).wait_send()
+
+
+def finish(w_in, m_in, v_in, kv_in, att_in, w_out, m_out, v_out, kv_out, att_out, state, kv, att, new_kv, out, sem):
+    def copy(src, dst, n):
+        return pltpu.make_async_copy(src, dst, sem.at[n])
+
+    loads = [copy(kv_in, kv, 0), copy(att_in, att, 1)]
+    moves = [copy(ref, state.at[n], 2 + n) for n, ref in enumerate((w_in, m_in, v_in))]
+    stores = [copy(state.at[n], ref, 5 + n) for n, ref in enumerate((w_out, m_out, v_out))]
+    for one in loads + moves:
+        one.start()
+    for one in loads:
+        one.wait()
     for s in range(STEPS):
         rows = slice(2 * s, 2 * s + 2)
-        out_ref[s] = att_ref[rows, :].astype(BF16)
+        out[s] = att[rows, :].astype(BF16)
         for n in range(2):
-            nkv_ref[n, s] = kv_ref[n, rows, :].astype(BF16)
+            new_kv[n, s] = kv[n, rows, :].astype(BF16)
+    small = [copy(new_kv, kv_out, 8), copy(out, att_out, 9)]
+    for one in small:
+        one.start()
+    for load, store in zip(moves, stores):
+        load.wait()
+        store.start()
+    for one in small + stores:
+        one.wait()
 
 
 def shards(
@@ -501,15 +566,18 @@
     anywhere = pl.BlockSpec(memory_space=pl.ANY)
     vmem = pl.BlockSpec(memory_space=pltpu.VMEM)
     dma = pltpu.SemaphoreType.DMA
-    grad, kv, att = pl.pallas_call(
+    like = jax.ShapeDtypeStruct((2 * OWN, HEAD), F32)
+    *updated, kv, att = pl.pallas_call(
         kernel,
         out_shape=(
-            jax.ShapeDtypeStruct((2 * OWN, HEAD), F32),
+            like,
+            like,
+            like,
             jax.ShapeDtypeStruct((2, PAD, HEAD), F32),
             jax.ShapeDtypeStruct((PAD, HEADS * HEAD), F32),
         ),
         in_specs=[anywhere] * 11,
-        out_specs=(anywhere, vmem, vmem),
+        out_specs=(anywhere,) * 3 + (vmem, vmem),
         scratch_shapes=[
             pltpu.VMEM((8, TOK, CHUNK), BF16),
             pltpu.VMEM((2 * TOK, HEAD), BF16),
@@ -528,14 +596,15 @@
             pltpu.VMEM((2, 2, OWN, HEAD), BF16),
             pltpu.VMEM((2, OWN, HEAD), BF16),
             pltpu.VMEM((2, OWN, HEAD), BF16),
-            pltpu.VMEM((16, 6 * PAD, HEAD), BF16),
-            pltpu.VMEM((16, 6 * PAD, HEAD), BF16),
-            pltpu.VMEM((8, 6 * PAD, HEAD), BF16),
-            pltpu.VMEM((42 * PAD, HEAD), F32),
+            pltpu.VMEM((16, ROWS, HEAD), F32),
+            pltpu.VMEM((16, ROWS, HEAD), BF16),
+            pltpu.VMEM((16, ROWS, HEAD), BF16),
+            pltpu.VMEM((8, ROWS, HEAD), BF16),
+            pltpu.VMEM((8, ROWS, HEAD), F32),
             pltpu.VMEM((PAD, WIDTH), F32),
             pltpu.VMEM((PAD, HEADS * HEAD), F32),
-            pltpu.VMEM((16, 4 * PAD, HEAD), BF16),
-            pltpu.VMEM((16, 4 * PAD, HEAD), BF16),
+            pltpu.VMEM((16, ROWS, HEAD), BF16),
+            pltpu.VMEM((16, ROWS, HEAD), F32),
             pltpu.VMEM((3 * HEAD, 2 * HEAD), BF16),
             pltpu.VMEM((16, 2 * PAD, HEAD), BF16),
             pltpu.VMEM((16, 2 * PAD, HEAD), BF16),
@@ -543,8 +612,8 @@
             pltpu.VMEM((WIDTH // HEAD, HEAD), F32),
             pltpu.VMEM((STEPS, 32), jnp.int32),
             pltpu.SMEM((2,), jnp.int32),
-            pltpu.VMEM((2 * OWN, HEAD), F32),
-            dma((19,)),
+            pltpu.VMEM((3, 2 * OWN, HEAD), F32),
+            dma((22,)),
             dma((2, 4)),
             dma((2, 2, 2, 2)),
             dma((2, 2, 2)),
@@ -569,7 +638,6 @@
         token_ids.T,
         lengths,
     )
-    like = jax.ShapeDtypeStruct((2 * OWN, HEAD), F32)
     *updated, new_kv, attended = pl.pallas_call(
         finish,
         out_shape=(
@@ -579,10 +647,18 @@
             jax.ShapeDtypeStruct((2, STEPS, 2, HEAD), BF16),
             jax.ShapeDtypeStruct((STEPS, 2, HEADS * HEAD), BF16),
         ),
-        in_specs=[vmem] * 6,
-        out_specs=(vmem,) * 5,
+        in_specs=[anywhere] * 5,
+        out_specs=(anywhere,) * 5,
+        scratch_shapes=[
+            pltpu.VMEM((3, 2 * OWN, HEAD), F32),
+            pltpu.VMEM((2, PAD, HEAD), F32),
+            pltpu.VMEM((PAD, HEADS * HEAD), F32),
+            pltpu.VMEM((2, STEPS, 2, HEAD), BF16),
+            pltpu.VMEM((STEPS, 2, HEADS * HEAD), BF16),
+            dma((10,)),
+        ],
         name="finish",
-    )(*state, grad, kv, att)
+    )(*updated, kv, att)
     new_weight, new_moment, new_second = (one.reshape(OWN, 2, HEAD) for one in updated)
     new_kv = new_kv.transpose(0, 2, 1, 3).reshape(2, rows, 1, STEPS, HEAD)
     attended = attended.transpose(1, 0, 2)

time: 36.4 us -> 35.9 us (0.986)
  Pallas kernels: 35.7 us -> 35.1 us
    pallas_call x1, Pallas kernels: 2.45 us -> 2.04 us  [shards(): pl.pallas_call(finish, out_shape=(like, like, like, jax.ShapeDtypeStruct(...]
where the time goes in v4:
time: 35.9 us; the launch traced here: 35.8 us
  Pallas kernels  35.1 us (98%)
  between operations  0.64 us (2%)
    pallas_call x1, Pallas kernels, shards(): pl.pallas_call(kernel, out_shape=(like, like, like, jax.ShapeDtypeStruct(...  33.1 us
    pallas_call x1, Pallas kernels, shards(): pl.pallas_call(finish, out_shape=(like, like, like, jax.ShapeDtypeStruct(...  2.04 us

profile of v4, /device:TPU:1, one launch (start us, length us, event | category | flops | bytes accessed | tf_op | source)
XLA Modules:
  0.0 35.8 jit_solution(17993009168159348570)
XLA Ops:
  0.6 33.1 %step.1 = (f32[640,128]{1,0:T(8,128)}, f32[640,128]{1,0:T(8,128)}, f32[640,128]{1,0:T(8,128)}, f32[2,8,128]{2,1,0:T(8,128)}, f32[8,1024]{1,0:T(8,128)}) custom-call(bf16[1024,5120]{1,0:T(8,128)(2,1)} %li_hbm.1, bf16[2048,128]{1,0:T(8,128)(2,1)} %bitcast.17, f32[640,128]{1,0:T(8,128)} %bitcast.18, f32[640,128]{1,0:T(8,128)} %bitcast.19, f32[640,128]{1,0:T(8,128)} %bitcast.20, ...), custom_call_target="tpu_custom_call" | custom-call | tf_op jit(solution)/shard_map/step/pallas_call | solution.py:570
  33.7 2.0 %finish.1 = (f32[640,128]{1,0:T(8,128)}, f32[640,128]{1,0:T(8,128)}, f32[640,128]{1,0:T(8,128)}, bf16[2,3,2,128]{3,2,1,0:T(2,128)(2,1)}, bf16[3,2,1024]{2,1,0:T(2,128)(2,1)}) custom-call(f32[640,128]{1,0:T(8,128)} %get-tuple-element.15.w_in, f32[640,128]{1,0:T(8,128)} %get-tuple-element.16.m_in, f32[640,128]{1,0:T(8,128)} %get-tuple-element.17.v_in, ...), custom_call_target="tpu_custom_call" | custom-call | tf_op jit(solution)/shard_map/finish/pallas_call | solution.py:641

commit v5 on v4

--- a/solution.py
+++ b/solution.py
@@ -350,7 +350,7 @@
     for ab in range(2):
         send3[ab] = x_sum(ab, 0).astype(BF16)
         step3(ab).start()
-    for d in (1, 7, 2, 6, 3, 5, 4):
+    for d in (2, 6, 1, 7, 4, 3, 5):
         e2_arrival(d).wait_recv()
         e3_go(d)
     step2_go(1)

time: 35.9 us -> 35.8 us (level)
  no operation moved by 1% of the time
where the time goes in v5:
time: 35.8 us; the launch traced here: 35.6 us
  Pallas kernels  35 us (98%)
  between operations  0.64 us (2%)
    pallas_call x1, Pallas kernels, shards(): pl.pallas_call(kernel, out_shape=(like, like, like, jax.ShapeDtypeStruct(...  32.9 us
    pallas_call x1, Pallas kernels, shards(): pl.pallas_call(finish, out_shape=(like, like, like, jax.ShapeDtypeStruct(...  2.04 us

profile of v5, /device:TPU:1, one launch (start us, length us, event | category | flops | bytes accessed | tf_op | source)
XLA Modules:
  0.0 35.6 jit_solution(15395981703404594179)
XLA Ops:
  0.6 32.9 %step.1 = (f32[640,128]{1,0:T(8,128)}, f32[640,128]{1,0:T(8,128)}, f32[640,128]{1,0:T(8,128)}, f32[2,8,128]{2,1,0:T(8,128)}, f32[8,1024]{1,0:T(8,128)}) custom-call(bf16[1024,5120]{1,0:T(8,128)(2,1)} %li_hbm.1, bf16[2048,128]{1,0:T(8,128)(2,1)} %bitcast.17, f32[640,128]{1,0:T(8,128)} %bitcast.18, f32[640,128]{1,0:T(8,128)} %bitcast.19, f32[640,128]{1,0:T(8,128)} %bitcast.20, ...), custom_call_target="tpu_custom_call" | custom-call | tf_op jit(solution)/shard_map/step/pallas_call | solution.py:570
  33.6 2.0 %finish.1 = (f32[640,128]{1,0:T(8,128)}, f32[640,128]{1,0:T(8,128)}, f32[640,128]{1,0:T(8,128)}, bf16[2,3,2,128]{3,2,1,0:T(2,128)(2,1)}, bf16[3,2,1024]{2,1,0:T(2,128)(2,1)}) custom-call(f32[640,128]{1,0:T(8,128)} %get-tuple-element.15.w_in, f32[640,128]{1,0:T(8,128)} %get-tuple-element.16.m_in, f32[640,128]{1,0:T(8,128)} %get-tuple-element.17.v_in, ...), custom_call_target="tpu_custom_call" | custom-call | tf_op jit(solution)/shard_map/finish/pallas_call | solution.py:641

commit v6 on v5

--- a/solution.py
+++ b/solution.py
@@ -449,12 +449,8 @@
         step3(ab).wait_recv()
         total = total + recv3[ab].astype(F32)
         every = pl.ds(ab, OWN, 2)
-        new_weight, new_moment, new_second = adam(
-            wm[0, every, :], wm[1, every, :], wm[2, every, :], total
-        )
-        updated[0, every, :] = new_weight
-        updated[1, every, :] = new_moment
-        updated[2, every, :] = new_second
+        new_weight, _, _ = adam(wm[0, every, :], wm[1, every, :], wm[2, every, :], total)
+        updated[0, every, :] = total
         fresh[pl.ds(pl.multiple_of(h * 64, 64), OWN), pl.ds(ab * HEAD, HEAD)] = new_weight.astype(
             BF16
         )
@@ -468,6 +464,7 @@
         kv_send[n] = jnp.concatenate([rows[:, :HEAD], rows[:, HEAD:]], axis=0).astype(BF16)
     for d in range(1, 16):
         kv(d).start()
+    updated[0], updated[1], updated[2] = adam(wm[0], wm[1], wm[2], updated[0])
     stores = [load(updated.at[n], ref, 18 + n) for n, ref in enumerate((nw_hbm, nm_hbm, nv_hbm))]
     for one in stores:
         one.start()

time: 35.8 us -> 35.8 us (level)
  no operation moved by 1% of the time
where the time goes in v6:
time: 35.8 us; the launch traced here: 35.6 us
  Pallas kernels  35 us (98%)
  between operations  0.64 us (2%)
    pallas_call x1, Pallas kernels, shards(): pl.pallas_call(kernel, out_shape=(like, like, like, jax.ShapeDtypeStruct(...  32.9 us
    pallas_call x1, Pallas kernels, shards(): pl.pallas_call(finish, out_shape=(like, like, like, jax.ShapeDtypeStruct(...  2.04 us

profile of v6, /device:TPU:1, one launch (start us, length us, event | category | flops | bytes accessed | tf_op | source)
XLA Modules:
  0.0 35.6 jit_solution(4088368623928220961)
XLA Ops:
  0.6 32.9 %step.1 = (f32[640,128]{1,0:T(8,128)}, f32[640,128]{1,0:T(8,128)}, f32[640,128]{1,0:T(8,128)}, f32[2,8,128]{2,1,0:T(8,128)}, f32[8,1024]{1,0:T(8,128)}) custom-call(bf16[1024,5120]{1,0:T(8,128)(2,1)} %li_hbm.1, bf16[2048,128]{1,0:T(8,128)(2,1)} %bitcast.17, f32[640,128]{1,0:T(8,128)} %bitcast.18, f32[640,128]{1,0:T(8,128)} %bitcast.19, f32[640,128]{1,0:T(8,128)} %bitcast.20, ...), custom_call_target="tpu_custom_call" | custom-call | tf_op jit(solution)/shard_map/step/pallas_call | solution.py:567
  33.6 2.0 %finish.1 = (f32[640,128]{1,0:T(8,128)}, f32[640,128]{1,0:T(8,128)}, f32[640,128]{1,0:T(8,128)}, bf16[2,3,2,128]{3,2,1,0:T(2,128)(2,1)}, bf16[3,2,1024]{2,1,0:T(2,128)(2,1)}) custom-call(f32[640,128]{1,0:T(8,128)} %get-tuple-element.15.w_in, f32[640,128]{1,0:T(8,128)} %get-tuple-element.16.m_in, f32[640,128]{1,0:T(8,128)} %get-tuple-element.17.v_in, ...), custom_call_target="tpu_custom_call" | custom-call | tf_op jit(solution)/shard_map/finish/pallas_call | solution.py:638
